TPU v7x, 256 devices: a whole 4x4x8 slice. The times are simulated.
256 devices in a mesh: role: 2 (over z_hi), grp: 4 (over z_lo), tp: 32 (over y, x, core).
Axes of the slice: x: 4, y: 4, z: 8 (z_hi: 2, z_lo: 4; z = z_hi * 4 + z_lo), core: 2. Of those that a mesh axis runs over, the one named last changes fastest.
Arguments:
- hidden: bfloat16 [4, 4, 16384], P(None, 'grp'), may hold values from -6 to 6
- current_weight: bfloat16 [16384, 16384], P(None, ('role', 'tp')), may hold values from -0.046875 to 0.046875
- down_factors: bfloat16 [2, 4, 16384, 64], P('role', 'grp', 'tp'), may hold values from -0.046875 to 0.046875
- up_factors: bfloat16 [2, 4, 64, 16384], P(None, 'grp', None, ('role', 'tp')), may hold values from -0.75 to 0.75
- cache: bfloat16 [4, 8192, 2, 1024], P('grp', ('role', 'tp')), may hold values from -360 to 360
- step_key_value: bfloat16 [4, 4, 2, 1024], P(None, 'grp'), may hold values from -6 to 6
- lengths: int32 [4], P('grp'), may hold values from 1024 to 8192
Outputs:
- attended: bfloat16 [4, 4, 16384], P(None, 'grp', ('role', 'tp'))
All inputs are finite; a program needn't handle non-finite values.
Results may differ from a plain program's by a relative error of at most 0.039.
Values may be sent and summed in bfloat16 or wider, within the bound.
No kernel may reach another device: no remote copies, remote signals or barrier semaphores. Data moves between devices by JAX's collectives and lax.ppermute only.
A program may use at most 128 MiB of HBM per device.

v0:
```python
import math

import jax
import jax.numpy as jnp
from jax import lax
from jax.sharding import PartitionSpec as P

MODEL_WIDTH = 16384
QUERY_HEADS = 128
KEY_VALUE_HEADS = 8
HEAD_WIDTH = 128
DECODE_STEPS = 4


def swapped(block, axis, apart):
    count = lax.axis_size(axis)
    route = []
    for low in range(count):
        high = low | 1 << apart
        if high != low and high < count:
            route += [(low, high), (high, low)]
    return lax.ppermute(block, axis, route)


def joined(x, axis, combine):
    everything = jax.tree.map(lambda part: lax.all_gather(part, axis), x)
    leading = jax.tree.map(lambda part: part[0], everything)

    def lap(k, so_far):
        return combine(so_far, jax.tree.map(lambda part: part[k], everything))

    return lax.fori_loop(1, lax.axis_size(axis), lap, leading)


def rotate(vec, pos):
    half = vec.shape[-1] // 2
    freq = jnp.exp(
        jnp.arange(half, dtype=jnp.float32) * (-2.0 * math.log(500000.0) / vec.shape[-1])
    )
    angle = pos.astype(jnp.float32)[..., None, None] * freq
    cosine = jnp.cos(angle)
    sine = jnp.sin(angle)
    first_product = vec[..., :half]
    second = vec[..., half:]
    return jnp.concatenate(
        [first_product * cosine - second * sine, second * cosine + first_product * sine], axis=-1
    )


def combine_parts(left_factor, right_factor):
    top = jnp.maximum(left_factor[0], right_factor[0])
    scale_left = jnp.exp(left_factor[0] - top)
    scale_right = jnp.exp(right_factor[0] - top)
    total = left_factor[1] * scale_left + right_factor[1] * scale_right
    row_indices = left_factor[2].shape[0]
    heads = left_factor[0].shape[1]
    summed = (
        left_factor[2].reshape(row_indices, heads, -1) * scale_left[..., None]
        + right_factor[2].reshape(row_indices, heads, -1) * scale_right[..., None]
    )
    return (top, total, summed.reshape(row_indices, -1))


def local(hidden, current_weight, down_factors, up_factors, cache, step_key_value, lengths):
    row_indices = hidden.shape[1]
    width = current_weight.shape[1]
    token_positions = cache.shape[1]
    group_share = QUERY_HEADS // KEY_VALUE_HEADS
    side = lax.axis_index("role")
    flat = lax.axis_index(("role", "tp"))
    first_side = side == 0
    group_down_factor = down_factors[0, 0]
    group_right_factor = jnp.concatenate([up_factors[0, 0], up_factors[1, 0]], axis=0).astype(
        jnp.float32
    )
    hidden_flat = hidden.reshape(DECODE_STEPS * row_indices, MODEL_WIDTH)
    whole_a = lax.all_gather(group_down_factor, "tp", axis=0, tiled=True)
    other_a = swapped(whole_a, "role", 0)
    new_a = jnp.where(first_side, whole_a, other_a)
    old_a = jnp.where(first_side, other_a, whole_a)
    left_factor = jnp.concatenate([new_a, -old_a], axis=1)
    merged = current_weight.astype(jnp.float32) + jnp.dot(
        left_factor.astype(jnp.float32), group_right_factor, precision=lax.Precision.HIGHEST
    )
    raw_all = jnp.dot(hidden_flat.astype(jnp.float32), merged, precision=lax.Precision.HIGHEST)
    raw_all = raw_all.reshape(DECODE_STEPS, row_indices, width // HEAD_WIDTH, HEAD_WIDTH)
    col_start = flat * width
    steps_pos = lengths[None, :] + jnp.arange(DECODE_STEPS, dtype=jnp.int32)[:, None]
    local_queries = (
        rotate(raw_all, steps_pos).reshape(DECODE_STEPS, row_indices, width).astype(jnp.bfloat16)
    )
    newest_token = (
        step_key_value[:, :, 0]
        .reshape(DECODE_STEPS, row_indices, KEY_VALUE_HEADS, HEAD_WIDTH)
        .astype(jnp.float32)
    )
    fresh_key = rotate(newest_token, steps_pos).astype(jnp.bfloat16)
    newest_value = (
        step_key_value[:, :, 1]
        .reshape(DECODE_STEPS, row_indices, KEY_VALUE_HEADS, HEAD_WIDTH)
        .astype(jnp.float32)
    )
    key_rows = cache[:, :, 0].reshape(row_indices, token_positions, KEY_VALUE_HEADS, HEAD_WIDTH)
    value_rows = (
        cache[:, :, 1]
        .reshape(row_indices, token_positions, KEY_VALUE_HEADS, HEAD_WIDTH)
        .astype(jnp.float32)
    )
    global_pos = flat * token_positions + jnp.arange(token_positions, dtype=jnp.int32)
    valid = (global_pos[None, :] < lengths[:, None])[:, None, None, :]
    holder = flat == 0
    scale = 1.0 / math.sqrt(HEAD_WIDTH)
    results = []
    for step_index in range(DECODE_STEPS):
        query_rows_all = lax.all_gather(
            local_queries[step_index], ("role", "tp"), axis=1, tiled=True
        )
        grouped_queries = query_rows_all.reshape(
            row_indices, KEY_VALUE_HEADS, group_share, HEAD_WIDTH
        )
        scores = (
            jnp.einsum(
                "rgqd,rpgd->rgqp", grouped_queries, key_rows, preferred_element_type=jnp.float32
            )
            * scale
        )
        fresh_scores = (
            jnp.einsum(
                "rgqd,srgd->rgqs", grouped_queries, fresh_key, preferred_element_type=jnp.float32
            )
            * scale
        )
        fresh_ok = ((jnp.arange(DECODE_STEPS) <= step_index) & holder)[None, None, None, :]
        top = jnp.maximum(
            jnp.max(jnp.where(valid, scores, -1e30), axis=-1),
            jnp.max(jnp.where(fresh_ok, fresh_scores, -1e30), axis=-1),
        )
        weights = jnp.where(valid, jnp.exp(scores - top[..., None]), 0.0)
        fresh_w = jnp.where(fresh_ok, jnp.exp(fresh_scores - top[..., None]), 0.0)
        total = (jnp.sum(weights, axis=-1) + jnp.sum(fresh_w, axis=-1)).reshape(
            row_indices, QUERY_HEADS
        )
        summed = jnp.einsum("rgqp,rpgd->rgqd", weights, value_rows) + jnp.einsum(
            "rgqs,srgd->rgqd", fresh_w, newest_value
        )
        top = top.reshape(row_indices, QUERY_HEADS)
        summed = summed.reshape(row_indices, QUERY_HEADS * HEAD_WIDTH)
        merged_top, merged_total, merged_sum = joined(
            (top, total, summed), ("role", "tp"), combine_parts
        )
        whole = merged_sum.reshape(row_indices, QUERY_HEADS, HEAD_WIDTH) / merged_total[..., None]
        out = lax.dynamic_slice_in_dim(
            whole.reshape(row_indices, QUERY_HEADS * HEAD_WIDTH), col_start, width, 1
        )
        results.append(out.astype(jnp.bfloat16))
    return jnp.stack(results, axis=0)


def solution(mesh):
    placed = (
        P(None, "grp", None),
        P(None, ("role", "tp")),
        P("role", "grp", "tp", None),
        P(None, "grp", None, ("role", "tp")),
        P("grp", ("role", "tp"), None, None),
        P(None, "grp", None, None),
        P("grp"),
    )
    return jax.shard_map(
        local, mesh=mesh, in_specs=placed, out_specs=P(None, "grp", ("role", "tp")), check_vma=False
    )
```

profile of v0, /device:TPU:32, one launch (start us, length us, event | category | flops | bytes accessed | tf_op | source)
XLA Modules:
  0.0 1806.6 jit_solution(8557072411853043321)
XLA Ops:
  7.3 54.9 %all-gather.15.cloned.1.call-done = bf16[1,1,16384,64]{2,3,1,0:T(8,128)(2,1)} async-done(((bf16[1,1,512,64]{2,3,1,0:T(8,128)(2,1)}), bf16[1,1,16384,64]{2,3,1,0:T(8,128)(2,1)}) %all-gather.15.cloned.1.call-update) | async-done | bytes 2097168 | tf_op jit(solution)/shard_map/all_gather | solution.py:77
  62.2 4.8 collective-permute-start
  67.7 2.2 fusion.99
  72.8 86.4 %collective-permute-done = bf16[16384,64]{0,1:T(8,128)(2,1)} collective-permute-done((bf16[16384,64]{0,1:T(8,128)(2,1)}, bf16[16384,64]{0,1:T(8,128)(2,1)}, u32[]{:S(2)}, u32[]{:S(2)}) %collective-permute-start) | collective-permute-done | bytes 2097184 | tf_op jit(solution)/shard_map/ppermute | solution.py:22
  159.2 3.8 broadcast_select_fusion
  163.0 6.4 convolution_add_fusion
  169.4 5.5 convolution_bitcast_fusion
  175.1 114.6 %all_gather.52 = bf16[1,16384]{1,0:T(2,128)(2,1)S(1)} all-gather(bf16[1,256]{1,0:T(2,128)(2,1)S(1)} %bitcast.322), channel_id=1, replica_groups=mesh['role'=2,'grp'=4,'tp'=32] {'role','tp'}, dimensions={1}, use_global_device_ids=true | all-gather | bytes 33280 | tf_op jit(solution)/shard_map/all_gather | solution.py:115
  291.6 110.2 %all_gather.64 = bf16[1,16384]{1,0:T(2,128)(2,1)S(1)} all-gather(bf16[1,256]{1,0:T(2,128)(2,1)S(1)} %bitcast.323), channel_id=1, replica_groups=mesh['role'=2,'grp'=4,'tp'=32] {'role','tp'}, dimensions={1}, use_global_device_ids=true | all-gather | bytes 33280 | tf_op jit(solution)/shard_map/all_gather | solution.py:115
  401.9 109.3 %all_gather.60 = bf16[1,16384]{1,0:T(2,128)(2,1)S(1)} all-gather(bf16[1,256]{1,0:T(2,128)(2,1)S(1)} %bitcast.324), channel_id=1, replica_groups=mesh['role'=2,'grp'=4,'tp'=32] {'role','tp'}, dimensions={1}, use_global_device_ids=true | all-gather | bytes 33280 | tf_op jit(solution)/shard_map/all_gather | solution.py:115
  511.4 107.8 %all_gather.56 = bf16[1,16384]{1,0:T(2,128)(2,1)S(1)} all-gather(bf16[1,256]{1,0:T(2,128)(2,1)S(1)} %bitcast.325), channel_id=1, replica_groups=mesh['role'=2,'grp'=4,'tp'=32] {'role','tp'}, dimensions={1}, use_global_device_ids=true | all-gather | bytes 33280 | tf_op jit(solution)/shard_map/all_gather | solution.py:115
  624.3 110.8 %all_gather.54 = f32[64,1,128]{2,1,0:T(1,128)S(1)} all-gather(f32[1,1,128]{2,1,0:T(1,128)S(1)} %add.360), channel_id=1, replica_groups=mesh['role'=2,'grp'=4,'tp'=32] {'role','tp'}, dimensions={0}, use_global_device_ids=true | all-gather | bytes 33280 | tf_op jit(solution)/shard_map/all_gather | solution.py:26
  735.1 107.9 %all_gather.53 = f32[64,1,128]{2,1,0:T(1,128)S(1)} all-gather(f32[1,1,128]{2,1,0:T(1,128)S(1)} %max.117), channel_id=1, replica_groups=mesh['role'=2,'grp'=4,'tp'=32] {'role','tp'}, dimensions={0}, use_global_device_ids=true | all-gather | bytes 33280 | tf_op jit(solution)/shard_map/all_gather | solution.py:26
  843.0 108.2 %all_gather.58 = f32[64,1,128]{2,1,0:T(1,128)S(1)} all-gather(f32[1,1,128]{2,1,0:T(1,128)S(1)} %add.364), channel_id=1, replica_groups=mesh['role'=2,'grp'=4,'tp'=32] {'role','tp'}, dimensions={0}, use_global_device_ids=true | all-gather | bytes 33280 | tf_op jit(solution)/shard_map/all_gather | solution.py:26
  951.2 107.8 %all_gather.57 = f32[64,1,128]{2,1,0:T(1,128)S(1)} all-gather(f32[1,1,128]{2,1,0:T(1,128)S(1)} %max.119), channel_id=1, replica_groups=mesh['role'=2,'grp'=4,'tp'=32] {'role','tp'}, dimensions={0}, use_global_device_ids=true | all-gather | bytes 33280 | tf_op jit(solution)/shard_map/all_gather | solution.py:26
  1058.9 108.2 %all_gather.62 = f32[64,1,128]{2,1,0:T(1,128)S(1)} all-gather(f32[1,1,128]{2,1,0:T(1,128)S(1)} %add.367), channel_id=1, replica_groups=mesh['role'=2,'grp'=4,'tp'=32] {'role','tp'}, dimensions={0}, use_global_device_ids=true | all-gather | bytes 33280 | tf_op jit(solution)/shard_map/all_gather | solution.py:26
  1167.1 107.8 %all_gather.61 = f32[64,1,128]{2,1,0:T(1,128)S(1)} all-gather(f32[1,1,128]{2,1,0:T(1,128)S(1)} %max.121), channel_id=1, replica_groups=mesh['role'=2,'grp'=4,'tp'=32] {'role','tp'}, dimensions={0}, use_global_device_ids=true | all-gather | bytes 33280 | tf_op jit(solution)/shard_map/all_gather | solution.py:26
  1274.9 108.2 %all_gather.66 = f32[64,1,128]{2,1,0:T(1,128)S(1)} all-gather(f32[1,1,128]{2,1,0:T(1,128)S(1)} %add.370), channel_id=1, replica_groups=mesh['role'=2,'grp'=4,'tp'=32] {'role','tp'}, dimensions={0}, use_global_device_ids=true | all-gather | bytes 33280 | tf_op jit(solution)/shard_map/all_gather | solution.py:26
  1383.0 107.8 %all_gather.65 = f32[64,1,128]{2,1,0:T(1,128)S(1)} all-gather(f32[1,1,128]{2,1,0:T(1,128)S(1)} %max.123), channel_id=1, replica_groups=mesh['role'=2,'grp'=4,'tp'=32] {'role','tp'}, dimensions={0}, use_global_device_ids=true | all-gather | bytes 33280 | tf_op jit(solution)/shard_map/all_gather | solution.py:26
  1492.9 75.9 %while.88 = (s32[]{:T(128)}, f32[1,128]{1,0:T(1,128)S(1)}, f32[1,128]{1,0:T(1,128)S(1)}, f32[1,16384]{1,0:T(1,128)S(1)}, f32[64,1,128]{2,1,0:T(1,128)S(1)}, /*in...) while((s32[]{:T(128)}, f32[1,128]{1,0:T(1,128)S(1)}, ...), condition=%wide.region_5.6_spmd, body=%wide.region_4.5_spmd.sunk | while | flops 50053 | bytes 466587 | solution.py:32
  1493.1 1.0 fusion.136
  1494.3 1.0 fusion.136
  1495.5 1.0 fusion.136
  1496.7 1.0 fusion.136
  1497.9 1.0 fusion.136
  1499.2 1.0 fusion.136
  1500.4 1.0 fusion.136
  1501.6 1.0 fusion.136
  1502.8 1.0 fusion.136
  1504.0 1.0 fusion.136
  1505.2 1.0 fusion.136
  1506.4 1.0 fusion.136
  1507.6 1.0 fusion.136
  1508.8 1.0 fusion.136
  1511.2 1.0 fusion.136
  1512.4 1.0 fusion.136
  1513.6 1.0 fusion.136
  1514.8 1.0 fusion.136
  1516.0 1.0 fusion.136
  1518.4 1.0 fusion.136
  1519.6 1.0 fusion.136
  1520.8 1.0 fusion.136
  1522.0 1.0 fusion.136
  1523.2 1.0 fusion.136
  1524.5 1.0 fusion.136
  1525.7 1.0 fusion.136
  1526.9 1.0 fusion.136
  1528.1 1.0 fusion.136
  1529.3 1.0 fusion.136
  1530.5 1.0 fusion.136
  1531.7 1.0 fusion.136
  1532.9 1.0 fusion.136
  1534.1 1.0 fusion.136
  1536.5 1.0 fusion.136
  1553.4 1.0 fusion.136
  1561.8 1.0 fusion.136
  1566.6 1.0 fusion.136
  1569.7 75.9 %while.89 = (s32[]{:T(128)}, f32[1,128]{1,0:T(1,128)S(1)}, f32[1,128]{1,0:T(1,128)S(1)}, f32[1,16384]{1,0:T(1,128)S(1)}, f32[64,1,128]{2,1,0:T(1,128)S(1)}, /*in...) while((s32[]{:T(128)}, f32[1,128]{1,0:T(1,128)S(1)}, ...), condition=%wide.region_11.12_spmd, body=%wide.region_10.11_spmd.sunk | while | flops 50053 | bytes 466587 | solution.py:32
  1571.1 1.0 fusion.139
  1574.7 1.0 fusion.139
  1576.0 1.0 fusion.139
  1579.6 1.0 fusion.139
  1646.5 75.9 %while.90 = (s32[]{:T(128)}, f32[1,128]{1,0:T(1,128)S(1)}, f32[1,128]{1,0:T(1,128)S(1)}, f32[1,16384]{1,0:T(1,128)S(1)}, f32[64,1,128]{2,1,0:T(1,128)S(1)}, /*in...) while((s32[]{:T(128)}, f32[1,128]{1,0:T(1,128)S(1)}, ...), condition=%wide.region_17.18_spmd, body=%wide.region_16.17_spmd.sunk | while | flops 50053 | bytes 466587 | solution.py:32
  1723.3 75.9 %while.91 = (s32[]{:T(128)}, f32[1,128]{1,0:T(1,128)S(1)}, f32[1,128]{1,0:T(1,128)S(1)}, f32[1,16384]{1,0:T(1,128)S(1)}, f32[64,1,128]{2,1,0:T(1,128)S(1)}, /*in...) while((s32[]{:T(128)}, f32[1,128]{1,0:T(1,128)S(1)}, ...), condition=%wide.region_23.24_spmd, body=%wide.region_22.23_spmd.sunk | while | flops 50053 | bytes 466587 | solution.py:32
  (1569 shorter events, 270.7 us)
Async XLA Ops:
  6.5 162.9 %copy-start = (bf16[4,1,16384]{2,0,1:T(4,128)(2,1)S(1)}, bf16[4,1,16384]{2,0,1:T(4,128)(2,1)}, u32[]{:S(2)}) copy-start(bf16[4,1,16384]{2,0,1:T(4,128)(2,1)} %param.15) | copy-start | bytes 393220
  6.5 55.7 %all-gather.15.cloned.1.call-start = ((), (), s32[]{:S(2)}) async-start(), calls=%async_computation.4 | async-start | bytes 2162688 | tf_op jit(solution)/shard_map/all_gather | solution.py:77
  7.3 1484.8 %all-gather.7.cloned.1.call-start = ((), (), s32[]{:S(2)}) async-start(), calls=%async_computation | async-start | bytes 4259840 | tf_op jit(solution)/shard_map/all_gather | solution.py:26
  62.2 97.0 %collective-permute-start = (bf16[16384,64]{0,1:T(8,128)(2,1)}, bf16[16384,64]{0,1:T(8,128)(2,1)}, u32[]{:S(2)}, u32[]{:S(2)}) collective-permute-start(bf16[16384,64]{0,1:T(8,128)(2,1)} %bitcast.300), channel_id=1, source_target_pairs={{0,128},{128,0},{1,129},{129,1},{2,130},{130,2},{3,131},{131,3},{4... | collective-permute-start | bytes 6291464 | tf_op jit(solution)/shard_map/ppermute | solution.py:22
  291.5 1277.4 %all-gather.9.cloned.1.call-start = ((), (), s32[]{:S(2)}) async-start(), calls=%async_computation.1 | async-start | bytes 4259840 | tf_op jit(solution)/shard_map/all_gather | solution.py:26
  621.4 1024.3 %all-gather.11.cloned.1.call-start = ((), (), s32[]{:S(2)}) async-start(), calls=%async_computation.2 | async-start | bytes 4259840 | tf_op jit(solution)/shard_map/all_gather | solution.py:26
  622.8 1099.6 %all-gather.13.cloned.1.call-start = ((), (), s32[]{:S(2)}) async-start(), calls=%async_computation.3 | async-start | bytes 4259840 | tf_op jit(solution)/shard_map/all_gather | solution.py:26
Sparse Core Ops, SparseCore 0:
  9.8 52.3 all-gather.14
  291.6 84.9 all-gather.6
  621.5 85.6 all-gather.8
  710.6 86.6 all-gather.10
  1492.2 93.3 all-gather.12
where the time goes:
time: 1830 us; the launch traced here: 1810 us
  blocking collectives  1310 us (72%)
  other arithmetic  263 us (14%)
  waiting for transfers between devices  142 us (8%)
  local copies, waits for them, and re-layouts  47 us (3%)
    all_gather x8, blocking collectives, joined(): everything = jax.tree.map(lambda part: lax.all_gather(part, axis), x)  867 us
    all_gather x4, blocking collectives, local(): lax.all_gather(local_queries[step_index], ('role', 'tp'), axis=1, tiled=T...  442 us
    add x252, other arithmetic, combine_parts(): left_factor[2].reshape(row_indices, heads, -1) * scale_left[..., None]  247 us
    ppermute x1, waiting for transfers between devices, swapped(): return lax.ppermute(block, axis, route)  86.4 us
    all_gather x1, waiting for transfers between devices, local(): whole_a = lax.all_gather(group_down_factor, 'tp', axis=0, tiled=True)  54.9 us
  transfers between devices with their start and end apart: 6, of which 2 were waited for; matrix products, arithmetic and copies ran while one was open for 13% of the time, Pallas kernels for 0%

commit v1 on v0

v1 whole, which is shorter than its diff:
```python
import math

import jax
import jax.numpy as jnp
from jax import lax
from jax.experimental import pallas as pl
from jax.experimental.pallas import tpu as pltpu
from jax.sharding import Mesh, PartitionSpec as P

QUERY_HEADS = 128
KEY_VALUE_HEADS = 8
HEAD_WIDTH = 128
DECODE_STEPS = 4
BLOCK_X = 4
BLOCK_CORE = 2
BLOCK = BLOCK_X * BLOCK_CORE
SHARE = QUERY_HEADS // KEY_VALUE_HEADS
ROWS = SHARE * DECODE_STEPS
MASKED = -1e30


def rotate(vec, pos):
    half = vec.shape[-1] // 2
    freq = jnp.exp(
        jnp.arange(half, dtype=jnp.float32) * (-2.0 * math.log(500000.0) / vec.shape[-1])
    )
    angle = pos.astype(jnp.float32)[..., None, None] * freq
    cosine = jnp.cos(angle)
    sine = jnp.sin(angle)
    first = vec[..., :half]
    second = vec[..., half:]
    turned = jnp.concatenate(
        [first * cosine - second * sine, second * cosine + first * sine], axis=-1
    )
    return turned, cosine, sine


def attend_kernel(info, lows, base, up, turn, cached, fresh, out, query):
    low = jnp.sum(lows[...], axis=0)
    high = low.astype(jnp.bfloat16).astype(jnp.float32)
    rest = low - high
    middle = rest.astype(jnp.bfloat16).astype(jnp.float32)
    terms = jnp.concatenate([high, middle, rest - middle, jnp.zeros_like(low)], axis=0).astype(
        jnp.bfloat16
    )
    cosine = turn[0]
    sine = turn[1]
    for j in range(BLOCK):
        extra = jnp.dot(terms, up[j], preferred_element_type=jnp.float32)
        raw = base[j] + ((extra[8:12] + extra[4:8]) + extra[0:4])
        for i in range(2):
            head = raw[:, i * HEAD_WIDTH : (i + 1) * HEAD_WIDTH]
            row = (2 * j + i) * DECODE_STEPS
            query[row : row + DECODE_STEPS, :] = head * cosine + pltpu.roll(head, 64, 1) * sine
    queries = query[...].astype(jnp.bfloat16)
    scale = 1.0 / math.sqrt(HEAD_WIDTH)
    length = info[0]
    place = info[1]
    n_src, pairs, _ = cached.shape
    column = lax.broadcasted_iota(jnp.int32, (ROWS, pairs), 1)
    row = lax.broadcasted_iota(jnp.int32, (ROWS, HEAD_WIDTH), 0)
    lane = lax.broadcasted_iota(jnp.int32, (ROWS, HEAD_WIDTH), 1)
    keyed = lax.rem(column, 2) == 0
    position = lax.div(column, 2)
    contract = (((1,), (1,)), ((), ()))
    masks = []
    scores = []
    for j in range(n_src):
        s = lax.dot_general(queries, cached[j], contract, preferred_element_type=jnp.float32)
        start = (j * BLOCK + place) * (pairs // 2)
        ok = keyed & (position + start < length)
        masks.append(ok)
        scores.append(jnp.where(ok, s * scale, MASKED))
    s = lax.dot_general(queries, fresh[...], contract, preferred_element_type=jnp.float32)
    ok = (lax.rem(lane, 2) == 0) & (lax.div(lane, 2) <= lax.rem(row, DECODE_STEPS)) & (place == 0)
    masks.append(ok)
    scores.append(jnp.where(ok, s * scale, MASKED))
    top = jnp.max(scores[-1], axis=-1, keepdims=True)
    for s in scores[:-1]:
        top = jnp.maximum(top, jnp.max(s, axis=-1, keepdims=True))
    total = jnp.zeros_like(top)
    summed = jnp.zeros((ROWS, HEAD_WIDTH), jnp.float32)
    for j in range(n_src + 1):
        weight = jnp.where(masks[j], jnp.exp(scores[j] - top), 0.0)
        total = total + jnp.sum(weight, axis=-1, keepdims=True)
        values = cached[j] if j < n_src else fresh[...]
        summed = summed + jnp.dot(
            pltpu.roll(weight, 1, 1).astype(jnp.bfloat16), values, preferred_element_type=jnp.float32
        )
    stats = jnp.where(lane < 64, top, total)
    each = 2 * DECODE_STEPS
    for d in range(BLOCK):
        out[d, :each, :] = summed[d * each : (d + 1) * each, :]
        out[d, each:, :] = stats[d * each : (d + 1) * each, :]


def combine_kernel(parts, out):
    each = 2 * DECODE_STEPS
    tops = [parts[d, each:, :][:, 0:1] for d in range(BLOCK)]
    totals = [parts[d, each:, :][:, 64:65] for d in range(BLOCK)]
    top = tops[0]
    for d in range(1, BLOCK):
        top = jnp.maximum(top, tops[d])
    total = jnp.zeros_like(top)
    summed = jnp.zeros((each, HEAD_WIDTH), jnp.float32)
    for d in range(BLOCK):
        factor = jnp.exp(tops[d] - top)
        total = total + totals[d] * factor
        summed = summed + parts[d, :each, :] * factor
    whole = summed / total
    out[...] = jnp.concatenate([whole[:DECODE_STEPS], whole[DECODE_STEPS:]], axis=1).astype(
        jnp.bfloat16
    )


def local(hidden, current_weight, down_factors, up_factors, cache, step_key_value, lengths):
    plane = ("y", "x", "core")
    block = ("x", "core")
    side = lax.axis_index("role")
    shard = lax.axis_index(plane)
    place = lax.axis_index(block)
    key_head = lax.axis_index(("role", "y"))
    rows = hidden.reshape(DECODE_STEPS, -1)
    down = down_factors[0, 0]
    part = jnp.dot(
        lax.dynamic_slice_in_dim(rows, shard * down.shape[0], down.shape[0], 1),
        down,
        preferred_element_type=jnp.float32,
    )
    blank = jnp.zeros_like(part)
    part = jnp.where(
        side == 0,
        jnp.concatenate([part, blank], axis=1),
        jnp.concatenate([blank, -part], axis=1),
    )
    everyone = ("role",) + plane
    lows = lax.all_to_all(
        jnp.broadcast_to(part, (lax.axis_size(everyone),) + part.shape), everyone, 0, 0
    )

    pairs = cache.shape[1] * 2
    sent = cache.reshape(pairs, KEY_VALUE_HEADS, HEAD_WIDTH).transpose(1, 0, 2)
    cached = lax.all_to_all(sent, ("role", "y"), 0, 0)

    up = up_factors.reshape(-1, up_factors.shape[-1])
    up = lax.all_to_all(jnp.broadcast_to(up, (BLOCK,) + up.shape), block, 0, 0)

    base = jnp.dot(rows, current_weight, preferred_element_type=jnp.float32)
    base = lax.all_to_all(jnp.broadcast_to(base, (BLOCK,) + base.shape), block, 0, 0)

    steps_pos = lengths[None, :] + jnp.arange(DECODE_STEPS, dtype=jnp.int32)[:, None]
    own = lax.dynamic_slice_in_dim(step_key_value, key_head * HEAD_WIDTH, HEAD_WIDTH, 3)
    fresh_key, cosine, sine = rotate(own[:, :, 0][:, :, None].astype(jnp.float32), steps_pos)
    cosine, sine = cosine[:, 0, 0], sine[:, 0, 0]
    turn = jnp.stack(
        [
            jnp.concatenate([cosine, cosine], axis=-1),
            jnp.concatenate([-sine, sine], axis=-1),
        ]
    )
    fresh = jnp.stack([fresh_key[:, 0, 0].astype(jnp.bfloat16), own[:, 0, 1]], axis=1)
    fresh = jnp.pad(
        fresh.reshape(2 * DECODE_STEPS, HEAD_WIDTH), ((0, HEAD_WIDTH - 2 * DECODE_STEPS), (0, 0))
    )
    info = jnp.concatenate([lengths, place[None].astype(jnp.int32)])

    vmem = pl.BlockSpec(memory_space=pltpu.VMEM)
    parts = pl.pallas_call(
        attend_kernel,
        out_shape=jax.ShapeDtypeStruct((BLOCK, 4 * DECODE_STEPS, HEAD_WIDTH), jnp.float32),
        in_specs=[pl.BlockSpec(memory_space=pltpu.SMEM)] + [vmem] * 6,
        out_specs=vmem,
        scratch_shapes=[pltpu.VMEM((ROWS, HEAD_WIDTH), jnp.float32)],
        compiler_params=pltpu.CompilerParams(vmem_limit_bytes=16 * 2**20),
        name="attend",
    )(info, lows, base, up, turn, cached, fresh)
    parts = lax.all_to_all(parts, block, 0, 0)
    out = pl.pallas_call(
        combine_kernel,
        out_shape=jax.ShapeDtypeStruct((DECODE_STEPS, 2 * HEAD_WIDTH), jnp.bfloat16),
        in_specs=[vmem],
        out_specs=vmem,
        name="combine",
    )(parts)
    return out[:, None, :]


def solution(mesh):
    role, grp, tp = mesh.devices.shape
    finer = Mesh(
        mesh.devices.reshape(role, grp, tp // BLOCK, BLOCK_X, BLOCK_CORE),
        ("role", "grp", "y", "x", "core"),
    )
    tp = ("y", "x", "core")
    both = ("role",) + tp
    placed = (
        P(None, "grp", None),
        P(None, both),
        P("role", "grp", tp, None),
        P(None, "grp", None, both),
        P("grp", both, None, None),
        P(None, "grp", None, None),
        P("grp"),
    )
    return jax.shard_map(
        local, mesh=finer, in_specs=placed, out_specs=P(None, "grp", both), check_vma=False
    )
```

time: 1830 us -> 90 us (0.05); the launches traced: 1810 us -> 89.5 us
  blocking collectives: 1310 us -> 34 us
  other arithmetic: 263 us -> 0.57 us
  waiting for transfers between devices: 142 us -> 30.4 us
  local copies, waits for them, and re-layouts: 47 us -> 4.42 us
    all_gather x12 -> x0, blocking collectives: 1310 us -> none  [the longest x8 867 us: joined(): everything = jax.tree.map(lambda part: lax.all_gather(part, axis), x)]
    add x256 -> x0, other arithmetic: 247 us -> none  [the longest x252 247 us: combine_parts(): left_factor[2].reshape(row_indices, heads, -1) * scale_left[..., None]]
    ppermute x1 -> x0, waiting for transfers between devices: 86.4 us -> none  [swapped(): return lax.ppermute(block, axis, route)]
    all_gather x5 -> x0, waiting for transfers between devices: 55 us -> none  [the longest x1 54.9 us: local(): whole_a = lax.all_gather(group_down_factor, 'tp', axis=0, tiled=True)]
    mul x504 -> x0, local copies, waits for them, and re-layouts: 38.3 us -> none  [the longest x252 19.7 us: combine_parts(): left_factor[2].reshape(row_indices, heads, -1) * scale_left[..., None]]
    all_to_all x0 -> x2, blocking collectives: none -> 34 us  [the longest x1 25.3 us: local(): lax.all_to_all(jnp.broadcast_to(part, (lax.axis_size(everyone),) + part.s...]
    all_to_all x0 -> x3, waiting for transfers between devices: none -> 30.4 us  [the longest x1 17.7 us: local(): cached = lax.all_to_all(sent, ('role', 'y'), 0, 0)]
  transfers between devices with their start and end apart: 6 -> 3, of which waited for: 2 -> 3; matrix products, arithmetic and copies ran while one was open for 13% -> 3% of each run, Pallas kernels for 0% -> 0%
where the time goes in v1:
time: 90 us; the launch traced here: 89.5 us
  blocking collectives  34 us (38%)
  waiting for transfers between devices  30.4 us (34%)
  starting transfers between devices  11.3 us (13%)
  matrix products  4.69 us (5%)
  local copies, waits for them, and re-layouts  4.42 us (5%)
  Pallas kernels  3.33 us (4%)
    all_to_all x1, blocking collectives, local(): lax.all_to_all(jnp.broadcast_to(part, (lax.axis_size(everyone),) + part.s...  25.3 us
    all_to_all x1, waiting for transfers between devices, local(): cached = lax.all_to_all(sent, ('role', 'y'), 0, 0)  17.7 us
    all_to_all x1, blocking collectives, local(): parts = lax.all_to_all(parts, block, 0, 0)  8.67 us
    all_to_all x1, waiting for transfers between devices, local(): up = lax.all_to_all(jnp.broadcast_to(up, (BLOCK,) + up.shape), block, 0, 0)  7.52 us
    all_to_all x1, waiting for transfers between devices, local(): lax.all_to_all(jnp.broadcast_to(base, (BLOCK,) + base.shape), block, 0, 0)  5.24 us
    dot_general x1, matrix products, local(): base = jnp.dot(rows, current_weight, preferred_element_type=jnp.float32)  4.57 us
    all_to_all x1, starting transfers between devices, local(): lax.all_to_all(jnp.broadcast_to(base, (BLOCK,) + base.shape), block, 0, 0)  4.3 us
    all_to_all x1, starting transfers between devices, local(): cached = lax.all_to_all(sent, ('role', 'y'), 0, 0)  3.49 us
  transfers between devices with their start and end apart: 3, of which 3 were waited for; matrix products, arithmetic and copies ran while one was open for 3% of the time, Pallas kernels for 0%

profile of v1, /device:TPU:32, one launch (start us, length us, event | category | flops | bytes accessed | tf_op | source)
XLA Modules:
  0.0 89.5 jit_solution(4695557174760712015)
XLA Ops:
  0.0 0.0 copy-start
  0.0 0.0 copy-start.3
  0.0 0.0 copy-start.2
  0.0 0.0 copy-start.1
  0.0 0.9 copy-done
  0.9 4.6 %fusion = f32[4,256]{1,0:T(4,128)S(1)} fusion(bf16[16384,256]{1,0:T(8,128)(2,1)} %param.8, bf16[4,1,16384]{2,0,1:T(4,128)(2,1)S(1)} %copy-done), kind=kOutput, calls=%fused_computation.1 | convolution fusion | flops 33554432 | bytes 8523776 | tf_op jit(solution)/shard_map/dot_general | solution.py:148
  5.5 0.6 broadcast_in_dim.22
  6.1 4.3 %all-to-all-start.1 = ((f32[8,4,256]{2,1,0:T(4,128)}), f32[8,4,256]{2,1,0:T(4,128)S(1)}, u32[]{:S(2)}, u32[]{:S(2)}) async-start(f32[8,4,256]{2,1,0:T(4,128)} %broadcast_in_dim.22), calls=%async_computation.1 | async-start | bytes 65536 | tf_op jit(solution)/shard_map/all_to_all | solution.py:149
  10.4 0.0 copy-done.3
  10.4 0.1 fusion.16
  10.5 0.1 pad_select_fusion
  10.6 5.2 %all-to-all-done.1.base = f32[8,4,256]{2,1,0:T(4,128)S(1)} async-done(((f32[8,4,256]{2,1,0:T(4,128)}), f32[8,4,256]{2,1,0:T(4,128)S(1)}, u32[]{:S(2)}, u32[]{:S(2)}) %all-to-all-start.1) | async-done | bytes 32800 | tf_op jit(solution)/shard_map/all_to_all | solution.py:149
  15.9 25.3 %all_to_all.25.lows = f32[64,4,128]{2,1,0:T(4,128)S(1)} all-to-all(f32[64,4,128]{2,1,0:T(4,128)S(1)} %broadcast_in_dim.21), channel_id=1, replica_groups=mesh['role'=2,'grp'=4,'y'=4,'x'=4,'core'=2] {'role','y','x','core'}, dimensions={0} | all-to-all | bytes 262144 | tf_op jit(solution)/shard_map/all_to_all | solution.py:137
  41.2 0.0 copy-done.2
  41.2 0.8 broadcast_in_dim.23
  42.0 3.5 %all-to-all-start.2 = ((bf16[8,128,256]{2,1,0:T(8,128)(2,1)}), bf16[8,128,256]{2,1,0:T(8,128)(2,1)S(1)}, u32[]{:S(2)}, u32[]{:S(2)}) async-start(bf16[8,128,256]{2,1,0:T(8,128)(2,1)} %broadcast_in_dim.23), calls=%async_computation.2 | async-start | bytes 1048576 | tf_op jit(solution)/shard_map/all_to_all | solution.py:146
  46.2 0.0 copy-done.1
  46.2 0.3 reshape.142
  46.6 0.9 copy.19
  47.4 0.8 constant_dynamic-slice_fusion
  48.3 7.5 %all-to-all-done.2.up = bf16[8,128,256]{2,1,0:T(8,128)(2,1)S(1)} async-done(((bf16[8,128,256]{2,1,0:T(8,128)(2,1)}), bf16[8,128,256]{2,1,0:T(8,128)(2,1)S(1)}, u32[]{:S(2)}, u32[]{:S(2)}) %all-to-all-start.2) | async-done | bytes 524320 | tf_op jit(solution)/shard_map/all_to_all | solution.py:146
  55.8 3.5 %all-to-all-start.3 = ((bf16[8,256,128]{2,1,0:T(8,128)(2,1)}), bf16[8,256,128]{2,1,0:T(8,128)(2,1)S(1)}, u32[]{:S(2)}, u32[]{:S(2)}) async-start(bf16[8,256,128]{2,1,0:T(8,128)(2,1)} %bitcast.29), calls=%async_computation.3 | async-start | bytes 1048576 | tf_op jit(solution)/shard_map/all_to_all | solution.py:143
  59.3 0.1 fusion.11
  59.4 0.1 maximum_bitcast_fusion.2
  59.5 0.1 pad_add_fusion.info
  59.6 0.1 multiply_cosine_fusion.1
  59.7 0.1 maximum_bitcast_fusion
  59.8 17.7 %all-to-all-done.3.cached = bf16[8,256,128]{2,1,0:T(8,128)(2,1)S(1)} async-done(((bf16[8,256,128]{2,1,0:T(8,128)(2,1)}), bf16[8,256,128]{2,1,0:T(8,128)(2,1)S(1)}, u32[]{:S(2)}, u32[]{:S(2)}) %all-to-all-start.3) | async-done | bytes 524320 | tf_op jit(solution)/shard_map/all_to_all | solution.py:143
  77.5 1.7 %attend.1 = f32[8,16,128]{2,1,0:T(8,128)S(1)} custom-call(s32[2]{0:T(128)S(1)} %pad_add_fusion.info, f32[64,4,128]{2,1,0:T(4,128)S(1)} %all_to_all.25.lows, f32[8,4,256]{2,1,0:T(4,128)S(1)} %all-to-all-done.1.base, bf16[8,128,256]{2,1,0:T(8,128)(2,1)S(1)} %all-to-all-done.2.up, f32[2,4,128]{2,1,0:T(4,128)S(1)} %pad_maximum_fusion.turn, ...), custom_call_target="tpu_custom_call" | custom-call | tf_op jit(solution)/shard_map/attend/pallas_call | solution.py:168
  79.2 8.7 %all_to_all.26.parts = f32[8,16,128]{2,1,0:T(8,128)} all-to-all(f32[8,16,128]{2,1,0:T(8,128)S(1)} %attend.1), channel_id=1, replica_groups=mesh['role'=2,'grp'=4,'y'=4,'x'=4,'core'=2] {'x','core'}, dimensions={0} | all-to-all | bytes 131072 | tf_op jit(solution)/shard_map/all_to_all | solution.py:177
  87.9 1.6 %combine.1 = bf16[4,256]{1,0:T(4,128)(2,1)} custom-call(f32[8,16,128]{2,1,0:T(8,128)} %all_to_all.26.parts), custom_call_target="tpu_custom_call" | custom-call | tf_op jit(solution)/shard_map/combine/pallas_call | solution.py:178
  (8 shorter events, 0.1 us)
Async XLA Ops:
  0.0 0.9 %copy-start = (bf16[4,1,16384]{2,0,1:T(4,128)(2,1)S(1)}, bf16[4,1,16384]{2,0,1:T(4,128)(2,1)}, u32[]{:S(2)}) copy-start(bf16[4,1,16384]{2,0,1:T(4,128)(2,1)} %param.7) | copy-start | bytes 393220
  0.0 10.4 %copy-start.3 = (bf16[1,1,512,64]{2,3,1,0:T(8,128)(2,1)S(1)}, bf16[1,1,512,64]{2,3,1,0:T(8,128)(2,1)}, u32[]{:S(2)}) copy-start(bf16[1,1,512,64]{2,3,1,0:T(8,128)(2,1)} %param.9) | copy-start | bytes 196612
  0.0 41.2 %copy-start.2 = (bf16[2,1,64,256]{3,2,1,0:T(8,128)(2,1)S(1)}, bf16[2,1,64,256]{3,2,1,0:T(8,128)(2,1)}, u32[]{:S(2)}) copy-start(bf16[2,1,64,256]{3,2,1,0:T(8,128)(2,1)} %param.10) | copy-start | bytes 196612
  0.0 46.2 %copy-start.1 = (bf16[1,128,2,1024]{3,2,1,0:T(2,128)(2,1)S(1)}, bf16[1,128,2,1024]{3,2,1,0:T(2,128)(2,1)}, u32[]{:S(2)}) copy-start(bf16[1,128,2,1024]{3,2,1,0:T(2,128)(2,1)} %param.11) | copy-start | bytes 1572868
  6.1 9.7 %all-to-all-start.1 = ((f32[8,4,256]{2,1,0:T(4,128)}), f32[8,4,256]{2,1,0:T(4,128)S(1)}, u32[]{:S(2)}, u32[]{:S(2)}) async-start(f32[8,4,256]{2,1,0:T(4,128)} %broadcast_in_dim.22), calls=%async_computation.1 | async-start | bytes 65536 | tf_op jit(solution)/shard_map/all_to_all | solution.py:149
  42.0 13.8 %all-to-all-start.2 = ((bf16[8,128,256]{2,1,0:T(8,128)(2,1)}), bf16[8,128,256]{2,1,0:T(8,128)(2,1)S(1)}, u32[]{:S(2)}, u32[]{:S(2)}) async-start(bf16[8,128,256]{2,1,0:T(8,128)(2,1)} %broadcast_in_dim.23), calls=%async_computation.2 | async-start | bytes 1048576 | tf_op jit(solution)/shard_map/all_to_all | solution.py:146
  55.8 21.7 %all-to-all-start.3 = ((bf16[8,256,128]{2,1,0:T(8,128)(2,1)}), bf16[8,256,128]{2,1,0:T(8,128)(2,1)S(1)}, u32[]{:S(2)}, u32[]{:S(2)}) async-start(bf16[8,256,128]{2,1,0:T(8,128)(2,1)} %bitcast.29), calls=%async_computation.3 | async-start | bytes 1048576 | tf_op jit(solution)/shard_map/all_to_all | solution.py:143

commit v2 on v1

v2 whole, which is shorter than its diff:
```python
import math

import jax
import jax.numpy as jnp
from jax import lax
from jax.experimental import pallas as pl
from jax.experimental.pallas import tpu as pltpu
from jax.sharding import Mesh, PartitionSpec as P

QUERY_HEADS = 128
KEY_VALUE_HEADS = 8
HEAD_WIDTH = 128
DECODE_STEPS = 4
BLOCK_X = 4
BLOCK_CORE = 2
BLOCK = BLOCK_X * BLOCK_CORE
SHARE = QUERY_HEADS // KEY_VALUE_HEADS
ROWS = SHARE * DECODE_STEPS
MASKED = -1e30


def angles(pos):
    half = HEAD_WIDTH // 2
    freq = jnp.exp(
        jnp.arange(half, dtype=jnp.float32) * (-2.0 * math.log(500000.0) / HEAD_WIDTH)
    )
    angle = pos.astype(jnp.float32)[:, None] * freq
    return jnp.cos(angle), jnp.sin(angle)


def swapped(block, axis, apart):
    count = lax.axis_size(axis)
    return lax.ppermute(block, axis, [(i, i ^ apart) for i in range(count)])


def split_kernel(info, hidden, down, cache, out):
    depth = down.shape[1]
    own = pl.ds(pl.multiple_of(info[0] * depth, depth), depth)
    part = lax.dot_general(
        hidden[:, own], down[...], (((1,), (1,)), ((), ())), preferred_element_type=jnp.float32
    )
    high = part.astype(jnp.bfloat16).astype(jnp.float32)
    middle = (part - high).astype(jnp.bfloat16).astype(jnp.float32)
    rest = part - high - middle
    terms = jnp.concatenate([high, middle], axis=1).astype(jnp.bfloat16)
    others = jnp.concatenate([rest, jnp.zeros_like(rest)], axis=1).astype(jnp.bfloat16)
    positions = cache.shape[0]
    for head in range(KEY_VALUE_HEADS):
        out[head, :positions] = cache[:, :, head * HEAD_WIDTH : (head + 1) * HEAD_WIDTH]
        out[head, positions:, 0, :] = terms
        out[head, positions:, 1, :] = others


def attend_kernel(info, message, up0, up1, up2, up3, turn, cached, newest, out, query):
    ups = (up0, up1, up2, up3)
    length = info[0]
    place = info[1]
    rank = up0.shape[0] // BLOCK_CORE
    low = jnp.sum(message[:, :, :rank], axis=0)
    high = low.astype(jnp.bfloat16).astype(jnp.float32)
    rest = low - high
    middle = rest.astype(jnp.bfloat16).astype(jnp.float32)
    terms = jnp.concatenate([high, middle, rest - middle, jnp.zeros_like(low)], axis=0).astype(
        jnp.bfloat16
    )
    cosine = turn[0]
    sine = turn[1]
    for j in range(BLOCK):
        up = ups[j // BLOCK_CORE][(j % BLOCK_CORE) * rank : (j % BLOCK_CORE + 1) * rank, :]
        extra = jnp.dot(terms, up, preferred_element_type=jnp.float32)
        raw = message[place ^ j][:, rank:] + ((extra[8:12] + extra[4:8]) + extra[0:4])
        for i in range(2):
            head = raw[:, i * HEAD_WIDTH : (i + 1) * HEAD_WIDTH]
            row = (2 * j + i) * DECODE_STEPS
            query[row : row + DECODE_STEPS, :] = head * cosine + pltpu.roll(head, 64, 1) * sine
    queries = query[...].astype(jnp.bfloat16)
    scale = 1.0 / math.sqrt(HEAD_WIDTH)
    own = pl.ds(pl.multiple_of(info[2] * HEAD_WIDTH, HEAD_WIDTH), HEAD_WIDTH)
    token = newest[:, 0, 0, own].astype(jnp.float32)
    token = token * cosine + pltpu.roll(token, 64, 1) * sine
    blank = jnp.zeros((HEAD_WIDTH - DECODE_STEPS, HEAD_WIDTH), jnp.float32)
    fresh_key = jnp.concatenate([token, blank], axis=0).astype(jnp.bfloat16)
    fresh_value = jnp.concatenate(
        [newest[:, 0, 1, own].astype(jnp.float32), blank], axis=0
    ).astype(jnp.bfloat16)
    n_src = cached.shape[0]
    pairs = cached.shape[1] - 2 * DECODE_STEPS
    column = lax.broadcasted_iota(jnp.int32, (ROWS, pairs), 1)
    row = lax.broadcasted_iota(jnp.int32, (ROWS, HEAD_WIDTH), 0)
    lane = lax.broadcasted_iota(jnp.int32, (ROWS, HEAD_WIDTH), 1)
    keyed = lax.rem(column, 2) == 0
    position = lax.div(column, 2)
    contract = (((1,), (1,)), ((), ()))
    masks = []
    scores = []
    for j in range(n_src):
        s = lax.dot_general(queries, cached[j, :pairs, :], contract, preferred_element_type=jnp.float32)
        start = (j * BLOCK + place) * (pairs // 2)
        ok = keyed & (position + start < length)
        masks.append(ok)
        scores.append(jnp.where(ok, s * scale, MASKED))
    s = lax.dot_general(queries, fresh_key, contract, preferred_element_type=jnp.float32)
    ok = (lane <= lax.rem(row, DECODE_STEPS)) & (place == 0)
    masks.append(ok)
    scores.append(jnp.where(ok, s * scale, MASKED))
    top = jnp.max(scores[-1], axis=-1, keepdims=True)
    for s in scores[:-1]:
        top = jnp.maximum(top, jnp.max(s, axis=-1, keepdims=True))
    total = jnp.zeros_like(top)
    summed = jnp.zeros((ROWS, HEAD_WIDTH), jnp.float32)
    for j in range(n_src + 1):
        weight = jnp.where(masks[j], jnp.exp(scores[j] - top), 0.0)
        total = total + jnp.sum(weight, axis=-1, keepdims=True)
        if j < n_src:
            weight, values = pltpu.roll(weight, 1, 1), cached[j, :pairs, :]
        else:
            values = fresh_value
        summed = summed + jnp.dot(
            weight.astype(jnp.bfloat16), values, preferred_element_type=jnp.float32
        )
    stats = jnp.where(lane < 64, top, total)
    each = 2 * DECODE_STEPS
    for d in range(BLOCK):
        out[place ^ d, :each, :] = summed[d * each : (d + 1) * each, :]
        out[place ^ d, each:, :] = stats[d * each : (d + 1) * each, :]


def combine(parts):
    each = 2 * DECODE_STEPS
    summed, stats = parts[:, :each], parts[:, each:]
    tops, totals = stats[:, :, :1], stats[:, :, 64:65]
    factor = jnp.exp(tops - jnp.max(tops, axis=0, keepdims=True))
    whole = jnp.sum(summed * factor, axis=0) / jnp.sum(totals * factor, axis=0)
    whole = whole.reshape(2, DECODE_STEPS, HEAD_WIDTH).swapaxes(0, 1)
    return whole.reshape(DECODE_STEPS, 2 * HEAD_WIDTH).astype(jnp.bfloat16)


def local(hidden, current_weight, down_factors, up_factors, cache, step_key_value, lengths):
    plane = ("y", "x", "core")
    block = ("x", "core")
    shard = lax.axis_index(plane)
    place = lax.axis_index(block)
    key_head = lax.axis_index(("role", "y"))
    rows = hidden.reshape(DECODE_STEPS, -1)
    down = down_factors[0, 0].T
    vmem = pl.BlockSpec(memory_space=pltpu.VMEM)
    smem = pl.BlockSpec(memory_space=pltpu.SMEM)
    positions = cache.shape[1]
    sent = pl.pallas_call(
        split_kernel,
        out_shape=jax.ShapeDtypeStruct(
            (KEY_VALUE_HEADS, positions + DECODE_STEPS, 2, HEAD_WIDTH), cache.dtype
        ),
        in_specs=[smem] + [vmem] * 3,
        out_specs=vmem,
        name="split",
    )(shard[None].astype(jnp.int32), rows, down, cache[0])
    cached = lax.all_to_all(sent, ("role", "y"), 0, 0)
    terms = cached[:, positions:].astype(jnp.float32)
    rank = down.shape[0]
    terms = (terms[:, :, 1, :rank] + terms[:, :, 0, rank:]) + terms[:, :, 0, :rank]
    terms = jnp.sum(terms.reshape(2, -1, DECODE_STEPS, rank), axis=1)
    low = jnp.concatenate([terms[0], -terms[1]], axis=1)
    cached = cached.reshape(KEY_VALUE_HEADS, -1, HEAD_WIDTH)

    up = up_factors.reshape(-1, up_factors.shape[-1])
    up = jnp.concatenate([up, swapped(up, "core", 1)], axis=0)
    ups = [up] + [swapped(up, "x", m) for m in range(1, BLOCK_X)]

    base = jnp.dot(rows, current_weight, preferred_element_type=jnp.float32)
    message = jnp.concatenate([low, base], axis=1)
    message = lax.all_to_all(jnp.broadcast_to(message, (BLOCK,) + message.shape), block, 0, 0)

    steps_pos = lengths[None, :] + jnp.arange(DECODE_STEPS, dtype=jnp.int32)[:, None]
    cosine, sine = angles(steps_pos[:, 0])
    turn = jnp.stack(
        [
            jnp.concatenate([cosine, cosine], axis=-1),
            jnp.concatenate([-sine, sine], axis=-1),
        ]
    )
    info = jnp.stack([lengths[0], place, key_head]).astype(jnp.int32)

    parts = pl.pallas_call(
        attend_kernel,
        out_shape=jax.ShapeDtypeStruct((BLOCK, 4 * DECODE_STEPS, HEAD_WIDTH), jnp.float32),
        in_specs=[smem] + [vmem] * 8,
        out_specs=vmem,
        scratch_shapes=[pltpu.VMEM((ROWS, HEAD_WIDTH), jnp.float32)],
        compiler_params=pltpu.CompilerParams(vmem_limit_bytes=16 * 2**20),
        name="attend",
    )(info, message, *ups, turn, cached, step_key_value)
    parts = lax.all_to_all(parts, block, 0, 0)
    out = combine(parts)
    return out[:, None, :]


def solution(mesh):
    role, grp, tp = mesh.devices.shape
    finer = Mesh(
        mesh.devices.reshape(role, grp, tp // BLOCK, BLOCK_X, BLOCK_CORE),
        ("role", "grp", "y", "x", "core"),
    )
    tp = ("y", "x", "core")
    both = ("role",) + tp
    placed = (
        P(None, "grp", None),
        P(None, both),
        P("role", "grp", tp, None),
        P(None, "grp", None, both),
        P("grp", both, None, None),
        P(None, "grp", None, None),
        P("grp"),
    )
    return jax.shard_map(
        local, mesh=finer, in_specs=placed, out_specs=P(None, "grp", both), check_vma=False
    )
```

time: 90 us -> 53.6 us (0.60)
  blocking collectives: 34 us -> 8 us
  waiting for transfers between devices: 30.4 us -> 14.3 us
  starting transfers between devices: 11.3 us -> 19.3 us
  local copies, waits for them, and re-layouts: 4.42 us -> 0.72 us
  other arithmetic: 0.57 us -> 1.58 us
    all_to_all x1 -> x0, blocking collectives: 25.3 us -> none  [local(): lax.all_to_all(jnp.broadcast_to(part, (lax.axis_size(everyone),) + part.s...]
    all_to_all x1, waiting for transfers between devices: 17.7 us -> 8.87 us  [local(): cached = lax.all_to_all(sent, ('role', 'y'), 0, 0)]
    all_to_all x2 -> x1, waiting for transfers between devices: 12.8 us -> 5.45 us  [local(): lax.all_to_all(jnp.broadcast_to(message, (BLOCK,) + message.shape), block...]
    all_to_all x1, starting transfers between devices: 3.49 us -> 10.2 us  [local(): cached = lax.all_to_all(sent, ('role', 'y'), 0, 0)]
    ppermute x0 -> x4, starting transfers between devices: none -> 4.79 us  [swapped(): return lax.ppermute(block, axis, [(i, i ^ apart) for i in range(count)])]
    all_to_all x2 -> x1, starting transfers between devices: 7.79 us -> 4.3 us  [local(): lax.all_to_all(jnp.broadcast_to(message, (BLOCK,) + message.shape), block...]
    reshape x2 -> x0, local copies, waits for them, and re-layouts: 1.22 us -> none  [local(): sent = cache.reshape(pairs, KEY_VALUE_HEADS, HEAD_WIDTH).transpose(1, 0, 2)]
  transfers between devices with their start and end apart: 3 -> 6, of which waited for: 3 -> 2; matrix products, arithmetic and copies ran while one was open for 3% -> 11% of each run, Pallas kernels for 0% -> 0%
where the time goes in v2:
time: 53.6 us; the launch traced here: 53.3 us
  starting transfers between devices  19.3 us (36%)
  waiting for transfers between devices  14.3 us (27%)
  blocking collectives  8 us (15%)
  matrix products  4.65 us (9%)
  Pallas kernels  4.02 us (7%)
  other arithmetic  1.58 us (3%)
  between operations  0.75 us (1%)
  local copies, waits for them, and re-layouts  0.72 us (1%)
    all_to_all x1, starting transfers between devices, local(): cached = lax.all_to_all(sent, ('role', 'y'), 0, 0)  10.2 us
    all_to_all x1, waiting for transfers between devices, local(): cached = lax.all_to_all(sent, ('role', 'y'), 0, 0)  8.87 us
    all_to_all x1, blocking collectives, local(): parts = lax.all_to_all(parts, block, 0, 0)  8 us
    all_to_all x1, waiting for transfers between devices, local(): lax.all_to_all(jnp.broadcast_to(message, (BLOCK,) + message.shape), block...  5.45 us
    ppermute x4, starting transfers between devices, swapped(): return lax.ppermute(block, axis, [(i, i ^ apart) for i in range(count)])  4.79 us
    dot_general x1, matrix products, local(): base = jnp.dot(rows, current_weight, preferred_element_type=jnp.float32)  4.65 us
    all_to_all x1, starting transfers between devices, local(): lax.all_to_all(jnp.broadcast_to(message, (BLOCK,) + message.shape), block...  4.3 us
    pallas_call x1, Pallas kernels, local(): pl.pallas_call(split_kernel, out_shape=jax.ShapeDtypeStruct((KEY_VALUE_HE...  2.39 us
  transfers between devices with their start and end apart: 6, of which 2 were waited for; matrix products, arithmetic and copies ran while one was open for 11% of the time, Pallas kernels for 0%

profile of v2, /device:TPU:32, one launch (start us, length us, event | category | flops | bytes accessed | tf_op | source)
XLA Modules:
  0.0 53.3 jit_solution(18419538360724355239)
XLA Ops:
  0.0 0.0 copy-start.1
  0.0 0.0 copy-start
  0.0 2.4 %split.1 = bf16[8,132,2,128]{3,2,1,0:T(2,128)(2,1)} custom-call(s32[1]{0:T(128)} %bitcast.2.info, bf16[4,16384]{1,0:T(4,128)(2,1)} %bitcast.30, bf16[64,512]{1,0:T(8,128)(2,1)} %bitcast.32, bf16[128,2,1024]{2,1,0:T(2,128)(2,1)} %bitcast.31), custom_call_target="tpu_custom_call" | custom-call | tf_op jit(solution)/shard_map/split/pallas_call | solution.py:149
  2.4 10.2 %all-to-all-start = ((bf16[8,132,2,128]{3,2,1,0:T(2,128)(2,1)}), bf16[8,132,2,128]{3,2,1,0:T(2,128)(2,1)S(1)}, u32[]{:S(2)}, u32[]{:S(2)}) async-start(bf16[8,132,2,128]{3,2,1,0:T(2,128)(2,1)} %split.1), calls=%async_computation | async-start | bytes 1081344 | tf_op jit(solution)/shard_map/all_to_all | solution.py:158
  12.6 0.0 collective-permute-start
  13.3 0.1 multiply_cosine_fusion
  13.4 0.1 maximum_bitcast_fusion
  13.5 4.6 %fusion.5 = f32[4,256]{1,0:T(4,128)S(1)} fusion(bf16[16384,256]{1,0:T(8,128)(2,1)} %param.8, bf16[4,1,16384]{2,0,1:T(4,128)(2,1)} %param.7), kind=kOutput, calls=%fused_computation.25 | convolution fusion | flops 33554432 | bytes 8523776 | tf_op jit(solution)/shard_map/dot_general | solution.py:170
  18.1 0.0 collective-permute-done
  18.1 0.0 copy-done.1
  18.2 1.6 %collective-permute-start.1 = (bf16[256,256]{1,0:T(8,128)(2,1)S(1)}, bf16[256,256]{1,0:T(8,128)(2,1)S(1)}, u32[]{:S(2)}, u32[]{:S(2)}) collective-permute-start(bf16[256,256]{1,0:T(8,128)(2,1)S(1)} %pad_maximum_fusion.up0), channel_id=1, source_target_pairs={{0,2},{2,0},{4,6},{6,4},{1,3},{3,1},{5,7},{7,5},{8,10},{10,8},{12,... | collective-permute-start | bytes 393224 | tf_op jit(solution)/shard_map/ppermute | solution.py:33
  19.8 2.7 %collective-permute-start.2 = (bf16[256,256]{1,0:T(8,128)(2,1)S(1)}, bf16[256,256]{1,0:T(8,128)(2,1)S(1)}, u32[]{:S(2)}, u32[]{:S(2)}) collective-permute-start(bf16[256,256]{1,0:T(8,128)(2,1)S(1)} %pad_maximum_fusion.up0), channel_id=1, source_target_pairs={{0,4},{2,6},{4,0},{6,2},{1,5},{3,7},{5,1},{7,3},{8,12},{10,14},{12... | collective-permute-start | bytes 393224 | tf_op jit(solution)/shard_map/ppermute | solution.py:33
  22.5 0.5 collective-permute-start.3
  23.0 8.9 %all-to-all-done = bf16[8,132,2,128]{3,2,1,0:T(2,128)(2,1)S(1)} async-done(((bf16[8,132,2,128]{3,2,1,0:T(2,128)(2,1)}), bf16[8,132,2,128]{3,2,1,0:T(2,128)(2,1)S(1)}, u32[]{:S(2)}, u32[]{:S(2)}) %all-to-all-start) | async-done | bytes 540704 | tf_op jit(solution)/shard_map/all_to_all | solution.py:158
  31.8 0.1 slice_add_fusion
  32.0 0.1 pad_maximum_fusion.1
  32.1 0.6 %broadcast_in_dim.5 = f32[8,4,384]{2,1,0:T(4,128)} broadcast(f32[4,384]{1,0:T(4,128)S(1)} %pad_maximum_fusion.1), dimensions={1,2} | broadcast | bytes 55296 | tf_op jit(solution)/shard_map/broadcast_in_dim | solution.py:172
  32.7 4.3 %all-to-all-start.1 = ((f32[8,4,384]{2,1,0:T(4,128)}), f32[8,4,384]{2,1,0:T(4,128)S(1)}, u32[]{:S(2)}, u32[]{:S(2)}) async-start(f32[8,4,384]{2,1,0:T(4,128)} %broadcast_in_dim.5), calls=%async_computation.1 | async-start | bytes 98304 | tf_op jit(solution)/shard_map/all_to_all | solution.py:172
  37.0 0.1 pad_add_fusion.info
  37.1 0.0 collective-permute-done.1.up1
  37.1 0.0 collective-permute-done.2.up2
  37.1 0.0 collective-permute-done.3.up3
  37.1 5.4 %all-to-all-done.1.message = f32[8,4,384]{2,1,0:T(4,128)S(1)} async-done(((f32[8,4,384]{2,1,0:T(4,128)}), f32[8,4,384]{2,1,0:T(4,128)S(1)}, u32[]{:S(2)}, u32[]{:S(2)}) %all-to-all-start.1) | async-done | bytes 49184 | tf_op jit(solution)/shard_map/all_to_all | solution.py:172
  42.5 0.0 copy-done
  42.5 1.6 %attend.1 = f32[8,16,128]{2,1,0:T(8,128)S(1)} custom-call(s32[3]{0:T(128)S(1)} %pad_add_fusion.info, f32[8,4,384]{2,1,0:T(4,128)S(1)} %all-to-all-done.1.message, bf16[256,256]{1,0:T(8,128)(2,1)S(1)} %pad_maximum_fusion.up0, bf16[256,256]{1,0:T(8,128)(2,1)S(1)} %collective-permute-done.1.up1, bf16[256,256]{1,0:T(8,128)(2,1)S(1)} %collective-permute-done.2.up2, ...), custom_call_target="tpu_custom_call" | custom-call | tf_op jit(solution)/shard_map/attend/pallas_call | solution.py:184
  44.2 8.0 %all_to_all.15 = f32[8,16,128]{2,1,0:T(8,128)S(1)} all-to-all(f32[8,16,128]{2,1,0:T(8,128)S(1)} %attend.1), channel_id=1, replica_groups=mesh['role'=2,'grp'=4,'y'=4,'x'=4,'core'=2] {'x','core'}, dimensions={0} | all-to-all | bytes 131072 | tf_op jit(solution)/shard_map/all_to_all | solution.py:193
  52.2 0.1 slice_reduce_fusion
  52.3 0.2 fusion
  52.5 0.1 div.11
  52.6 0.1 fusion.1
  52.7 0.7 %fusion.4 = bf16[4,1,256]{2,0,1:T(4,128)(2,1)} fusion(f32[2,4,128]{2,1,0:T(4,128)S(1)} %bitcast.36, f32[2,4]{1,0:T(2,128)S(1)} %div.11), kind=kLoop, calls=%fused_computation.21 | loop fusion | flops 2048 | bytes 6176 | tf_op jit(solution)/shard_map/convert_element_type | solution.py:135
  (7 shorter events, 0.1 us)
Async XLA Ops:
  0.0 18.1 %copy-start.1 = (bf16[2,1,64,256]{3,2,1,0:T(8,128)(2,1)S(1)}, bf16[2,1,64,256]{3,2,1,0:T(8,128)(2,1)}, u32[]{:S(2)}) copy-start(bf16[2,1,64,256]{3,2,1,0:T(8,128)(2,1)} %param.10) | copy-start | bytes 196612
  0.0 42.5 %copy-start = (bf16[4,1,2,1024]{3,2,1,0:T(2,128)(2,1)S(1)}, bf16[4,1,2,1024]{3,2,1,0:T(2,128)(2,1)}, u32[]{:S(2)}) copy-start(bf16[4,1,2,1024]{3,2,1,0:T(2,128)(2,1)} %newest.1) | copy-start | bytes 49156
  2.4 29.4 %all-to-all-start = ((bf16[8,132,2,128]{3,2,1,0:T(2,128)(2,1)}), bf16[8,132,2,128]{3,2,1,0:T(2,128)(2,1)S(1)}, u32[]{:S(2)}, u32[]{:S(2)}) async-start(bf16[8,132,2,128]{3,2,1,0:T(2,128)(2,1)} %split.1), calls=%async_computation | async-start | bytes 1081344 | tf_op jit(solution)/shard_map/all_to_all | solution.py:158
  12.6 5.5 %collective-permute-start = (bf16[128,256]{1,0:T(8,128)(2,1)}, bf16[128,256]{1,0:T(8,128)(2,1)S(1)}, u32[]{:S(2)}, u32[]{:S(2)}) collective-permute-start(bf16[128,256]{1,0:T(8,128)(2,1)} %bitcast.34), channel_id=1, source_target_pairs={{0,1},{1,0},{2,3},{3,2},{4,5},{5,4},{6,7},{7,6},{8,9},{9,8},{10,11... | collective-permute-start | bytes 196616 | tf_op jit(solution)/shard_map/ppermute | solution.py:33
  18.2 18.9 %collective-permute-start.1 = (bf16[256,256]{1,0:T(8,128)(2,1)S(1)}, bf16[256,256]{1,0:T(8,128)(2,1)S(1)}, u32[]{:S(2)}, u32[]{:S(2)}) collective-permute-start(bf16[256,256]{1,0:T(8,128)(2,1)S(1)} %pad_maximum_fusion.up0), channel_id=1, source_target_pairs={{0,2},{2,0},{4,6},{6,4},{1,3},{3,1},{5,7},{7,5},{8,10},{10,8},{12,... | collective-permute-start | bytes 393224 | tf_op jit(solution)/shard_map/ppermute | solution.py:33
  19.8 17.3 %collective-permute-start.2 = (bf16[256,256]{1,0:T(8,128)(2,1)S(1)}, bf16[256,256]{1,0:T(8,128)(2,1)S(1)}, u32[]{:S(2)}, u32[]{:S(2)}) collective-permute-start(bf16[256,256]{1,0:T(8,128)(2,1)S(1)} %pad_maximum_fusion.up0), channel_id=1, source_target_pairs={{0,4},{2,6},{4,0},{6,2},{1,5},{3,7},{5,1},{7,3},{8,12},{10,14},{12... | collective-permute-start | bytes 393224 | tf_op jit(solution)/shard_map/ppermute | solution.py:33
  22.5 14.6 %collective-permute-start.3 = (bf16[256,256]{1,0:T(8,128)(2,1)S(1)}, bf16[256,256]{1,0:T(8,128)(2,1)S(1)}, u32[]{:S(2)}, u32[]{:S(2)}) collective-permute-start(bf16[256,256]{1,0:T(8,128)(2,1)S(1)} %pad_maximum_fusion.up0), channel_id=1, source_target_pairs={{0,6},{2,4},{4,2},{6,0},{1,7},{3,5},{5,3},{7,1},{8,14},{10,12},{12... | collective-permute-start | bytes 393224 | tf_op jit(solution)/shard_map/ppermute | solution.py:33
  32.7 9.8 %all-to-all-start.1 = ((f32[8,4,384]{2,1,0:T(4,128)}), f32[8,4,384]{2,1,0:T(4,128)S(1)}, u32[]{:S(2)}, u32[]{:S(2)}) async-start(f32[8,4,384]{2,1,0:T(4,128)} %broadcast_in_dim.5), calls=%async_computation.1 | async-start | bytes 98304 | tf_op jit(solution)/shard_map/all_to_all | solution.py:172

commit v3 on v2

--- a/solution.py
+++ b/solution.py
@@ -33,30 +33,62 @@
     return lax.ppermute(block, axis, [(i, i ^ apart) for i in range(count)])
 
 
-def split_kernel(info, hidden, down, cache, out):
+SPLITS = 4
+
+
+def split_kernel(info, hidden, down, cache, out, some, factor, held, ready, sems):
+    positions = cache.shape[0]
+    piece = positions // SPLITS
     depth = down.shape[1]
     own = pl.ds(pl.multiple_of(info[0] * depth, depth), depth)
+    fetches = [
+        pltpu.make_async_copy(hidden.at[:, own], some, sems.at[0]),
+        pltpu.make_async_copy(down, factor, sems.at[1]),
+    ]
+    for k in range(SPLITS):
+        rows = pl.ds(k * piece, piece)
+        fetches.append(pltpu.make_async_copy(cache.at[rows], held.at[rows], sems.at[2 + k]))
+    for fetch in fetches:
+        fetch.start()
+    stores = []
+    for k in range(SPLITS):
+        fetches[2 + k].wait()
+        rows = slice(k * piece, (k + 1) * piece)
+        for head in range(KEY_VALUE_HEADS):
+            columns = slice(head * HEAD_WIDTH, (head + 1) * HEAD_WIDTH)
+            ready[head, rows] = held[rows, :, columns]
+        rows = pl.ds(k * piece, piece)
+        stores.append(
+            pltpu.make_async_copy(ready.at[:, rows], out.at[:, rows], sems.at[2 + SPLITS + k])
+        )
+        stores[-1].start()
+    fetches[0].wait()
+    fetches[1].wait()
     part = lax.dot_general(
-        hidden[:, own], down[...], (((1,), (1,)), ((), ())), preferred_element_type=jnp.float32
+        some[...], factor[...], (((1,), (1,)), ((), ())), preferred_element_type=jnp.float32
     )
     high = part.astype(jnp.bfloat16).astype(jnp.float32)
-    middle = (part - high).astype(jnp.bfloat16).astype(jnp.float32)
-    rest = part - high - middle
-    terms = jnp.concatenate([high, middle], axis=1).astype(jnp.bfloat16)
-    others = jnp.concatenate([rest, jnp.zeros_like(rest)], axis=1).astype(jnp.bfloat16)
-    positions = cache.shape[0]
+    terms = jnp.concatenate([high, part - high], axis=1).astype(jnp.bfloat16)
     for head in range(KEY_VALUE_HEADS):
-        out[head, :positions] = cache[:, :, head * HEAD_WIDTH : (head + 1) * HEAD_WIDTH]
-        out[head, positions:, 0, :] = terms
-        out[head, positions:, 1, :] = others
-
-
-def attend_kernel(info, message, up0, up1, up2, up3, turn, cached, newest, out, query):
+        for t in range(DECODE_STEPS):
+            ready[head, positions + t // 2, t % 2, :] = terms[t]
+    rows = pl.ds(positions, DECODE_STEPS // 2)
+    stores.append(
+        pltpu.make_async_copy(ready.at[:, rows], out.at[:, rows], sems.at[2 + 2 * SPLITS])
+    )
+    stores[-1].start()
+    for store in stores:
+        store.wait()
+
+
+def attend_kernel(
+    info, lows, up0, up1, up2, up3, turn, cached, newest, out, query
+):
     ups = (up0, up1, up2, up3)
     length = info[0]
     place = info[1]
-    rank = up0.shape[0] // BLOCK_CORE
-    low = jnp.sum(message[:, :, :rank], axis=0)
+    low = jnp.sum(lows[...], axis=0)
+    rank = low.shape[1]
     high = low.astype(jnp.bfloat16).astype(jnp.float32)
     rest = low - high
     middle = rest.astype(jnp.bfloat16).astype(jnp.float32)
@@ -66,9 +98,13 @@
     cosine = turn[0]
     sine = turn[1]
     for j in range(BLOCK):
-        up = ups[j // BLOCK_CORE][(j % BLOCK_CORE) * rank : (j % BLOCK_CORE + 1) * rank, :]
-        extra = jnp.dot(terms, up, preferred_element_type=jnp.float32)
-        raw = message[place ^ j][:, rank:] + ((extra[8:12] + extra[4:8]) + extra[0:4])
+        start = (j % BLOCK_CORE) * (up0.shape[0] // BLOCK_CORE)
+        both = ups[j // BLOCK_CORE]
+        extra = jnp.dot(
+            terms, both[start : start + rank, :], preferred_element_type=jnp.float32
+        )
+        base = both[start + rank : start + rank + 16, :].astype(jnp.float32)
+        raw = ((base[8:12] + base[4:8]) + base[0:4]) + ((extra[8:12] + extra[4:8]) + extra[0:4])
         for i in range(2):
             head = raw[:, i * HEAD_WIDTH : (i + 1) * HEAD_WIDTH]
             row = (2 * j + i) * DECODE_STEPS
@@ -84,7 +120,7 @@
         [newest[:, 0, 1, own].astype(jnp.float32), blank], axis=0
     ).astype(jnp.bfloat16)
     n_src = cached.shape[0]
-    pairs = cached.shape[1] - 2 * DECODE_STEPS
+    pairs = cached.shape[1] - DECODE_STEPS
     column = lax.broadcasted_iota(jnp.int32, (ROWS, pairs), 1)
     row = lax.broadcasted_iota(jnp.int32, (ROWS, HEAD_WIDTH), 0)
     lane = lax.broadcasted_iota(jnp.int32, (ROWS, HEAD_WIDTH), 1)
@@ -145,31 +181,42 @@
     down = down_factors[0, 0].T
     vmem = pl.BlockSpec(memory_space=pltpu.VMEM)
     smem = pl.BlockSpec(memory_space=pltpu.SMEM)
+    hbm = pl.BlockSpec(memory_space=pl.ANY)
     positions = cache.shape[1]
+    sent = jax.ShapeDtypeStruct(
+        (KEY_VALUE_HEADS, positions + DECODE_STEPS // 2, 2, HEAD_WIDTH), cache.dtype
+    )
     sent = pl.pallas_call(
         split_kernel,
-        out_shape=jax.ShapeDtypeStruct(
-            (KEY_VALUE_HEADS, positions + DECODE_STEPS, 2, HEAD_WIDTH), cache.dtype
-        ),
-        in_specs=[smem] + [vmem] * 3,
-        out_specs=vmem,
+        out_shape=sent,
+        in_specs=[smem] + [hbm] * 3,
+        out_specs=hbm,
+        scratch_shapes=[
+            pltpu.VMEM((rows.shape[0], down.shape[1]), rows.dtype),
+            pltpu.VMEM(down.shape, down.dtype),
+            pltpu.VMEM(cache.shape[1:], cache.dtype),
+            pltpu.VMEM(sent.shape, sent.dtype),
+            pltpu.SemaphoreType.DMA((3 + 2 * SPLITS,)),
+        ],
+        compiler_params=pltpu.CompilerParams(vmem_limit_bytes=58 * 2**20),
         name="split",
     )(shard[None].astype(jnp.int32), rows, down, cache[0])
     cached = lax.all_to_all(sent, ("role", "y"), 0, 0)
-    terms = cached[:, positions:].astype(jnp.float32)
     rank = down.shape[0]
-    terms = (terms[:, :, 1, :rank] + terms[:, :, 0, rank:]) + terms[:, :, 0, :rank]
-    terms = jnp.sum(terms.reshape(2, -1, DECODE_STEPS, rank), axis=1)
+    terms = cached[:, positions:].astype(jnp.float32).reshape(2, -1, DECODE_STEPS, 2, rank)
+    terms = jnp.sum(terms[:, :, :, 1] + terms[:, :, :, 0], axis=1)
     low = jnp.concatenate([terms[0], -terms[1]], axis=1)
+    lows = lax.all_to_all(jnp.broadcast_to(low, (BLOCK,) + low.shape), block, 0, 0)
     cached = cached.reshape(KEY_VALUE_HEADS, -1, HEAD_WIDTH)
 
-    up = up_factors.reshape(-1, up_factors.shape[-1])
+    base = jnp.dot(rows, current_weight, preferred_element_type=jnp.float32)
+    high = lax.reduce_precision(base, 8, 7)
+    middle = lax.reduce_precision(base - high, 8, 7)
+    parts = [high, middle, base - high - middle, jnp.zeros_like(base)]
+    parts = [term.astype(jnp.bfloat16) for term in parts]
+    up = jnp.concatenate([up_factors.reshape(-1, up_factors.shape[-1])] + parts, axis=0)
     up = jnp.concatenate([up, swapped(up, "core", 1)], axis=0)
     ups = [up] + [swapped(up, "x", m) for m in range(1, BLOCK_X)]
-
-    base = jnp.dot(rows, current_weight, preferred_element_type=jnp.float32)
-    message = jnp.concatenate([low, base], axis=1)
-    message = lax.all_to_all(jnp.broadcast_to(message, (BLOCK,) + message.shape), block, 0, 0)
 
     steps_pos = lengths[None, :] + jnp.arange(DECODE_STEPS, dtype=jnp.int32)[:, None]
     cosine, sine = angles(steps_pos[:, 0])
@@ -189,7 +236,7 @@
         scratch_shapes=[pltpu.VMEM((ROWS, HEAD_WIDTH), jnp.float32)],
         compiler_params=pltpu.CompilerParams(vmem_limit_bytes=16 * 2**20),
         name="attend",
-    )(info, message, *ups, turn, cached, step_key_value)
+    )(info, lows, *ups, turn, cached, step_key_value)
     parts = lax.all_to_all(parts, block, 0, 0)
     out = combine(parts)
     return out[:, None, :]

time: 53.6 us -> 53.2 us (level)
    ppermute x4, starting transfers between devices: 4.79 us -> 4.25 us  [swapped(): return lax.ppermute(block, axis, [(i, i ^ apart) for i in range(count)])]
  transfers between devices with their start and end apart: 6 -> 6, of which waited for: 2 -> 3; matrix products, arithmetic and copies ran while one was open for 11% -> 11% of each run, Pallas kernels for 0% -> 0%
where the time goes in v3:
time: 53.2 us; the launch traced here: 52.9 us
  starting transfers between devices  18.8 us (35%)
  waiting for transfers between devices  14.2 us (27%)
  blocking collectives  8 us (15%)
  matrix products  4.65 us (9%)
  Pallas kernels  3.9 us (7%)
  other arithmetic  1.49 us (3%)
  local copies, waits for them, and re-layouts  1.06 us (2%)
  between operations  0.77 us (1%)
    all_to_all x1, starting transfers between devices, local(): cached = lax.all_to_all(sent, ('role', 'y'), 0, 0)  10.2 us
    all_to_all x1, waiting for transfers between devices, local(): cached = lax.all_to_all(sent, ('role', 'y'), 0, 0)  8.78 us
    all_to_all x1, blocking collectives, local(): parts = lax.all_to_all(parts, block, 0, 0)  8 us
    all_to_all x1, waiting for transfers between devices, local(): lax.all_to_all(jnp.broadcast_to(low, (BLOCK,) + low.shape), block, 0, 0)  5.08 us
    dot_general x1, matrix products, local(): base = jnp.dot(rows, current_weight, preferred_element_type=jnp.float32)  4.65 us
    all_to_all x1, starting transfers between devices, local(): lax.all_to_all(jnp.broadcast_to(low, (BLOCK,) + low.shape), block, 0, 0)  4.3 us
    ppermute x4, starting transfers between devices, swapped(): return lax.ppermute(block, axis, [(i, i ^ apart) for i in range(count)])  4.25 us
    pallas_call x1, Pallas kernels, local(): pl.pallas_call(split_kernel, out_shape=sent, in_specs=[smem] + [hbm] * 3,...  2.27 us
  transfers between devices with their start and end apart: 6, of which 3 were waited for; matrix products, arithmetic and copies ran while one was open for 11% of the time, Pallas kernels for 0%

profile of v3, /device:TPU:32, one launch (start us, length us, event | category | flops | bytes accessed | tf_op | source)
XLA Modules:
  0.0 52.9 jit_solution(7513551086509810063)
XLA Ops:
  0.0 0.0 copy-start.1
  0.0 0.0 copy-start
  0.0 2.3 %split.1 = bf16[8,130,2,128]{3,2,1,0:T(2,128)(2,1)} custom-call(s32[1]{0:T(128)} %bitcast.2.info, bf16[4,16384]{1,0:T(4,128)(2,1)} %bitcast.31, bf16[64,512]{1,0:T(8,128)(2,1)} %bitcast.35, bf16[128,2,1024]{2,1,0:T(2,128)(2,1)} %bitcast.32), custom_call_target="tpu_custom_call" | custom-call | tf_op jit(solution)/shard_map/split/pallas_call | solution.py:189
  2.3 10.2 %all-to-all-start = ((bf16[8,130,2,128]{3,2,1,0:T(2,128)(2,1)}), bf16[8,130,2,128]{3,2,1,0:T(2,128)(2,1)S(1)}, u32[]{:S(2)}, u32[]{:S(2)}) async-start(bf16[8,130,2,128]{3,2,1,0:T(2,128)(2,1)} %split.1), calls=%async_computation | async-start | bytes 1064960 | tf_op jit(solution)/shard_map/all_to_all | solution.py:204
  12.5 4.6 %fusion.4 = (bf16[4,256]{1,0:T(4,128)(2,1)S(1)}, bf16[4,256]{1,0:T(4,128)(2,1)S(1)}, bf16[4,256]{1,0:T(4,128)(2,1)S(1)}) fusion(bf16[16384,256]{1,0:T(8,128)(2,1)} %param.8, bf16[4,1,16384]{2,0,1:T(4,128)(2,1)} %param.7), kind=kOutput, calls=%fused_computation.14 | convolution fusion | flops 33561600 | bytes 8525824 | tf_op jit(solution)/shard_map/dot_general | solution.py:212
  17.2 0.0 copy-done.1
  17.2 0.1 concatenate.17
  17.2 0.1 collective-permute-start
  18.0 0.1 multiply_cosine_fusion
  18.1 0.1 maximum_bitcast_fusion
  18.2 0.4 collective-permute-done
  18.6 0.1 concatenate.18.up0
  18.6 2.8 %collective-permute-start.3 = (bf16[288,256]{1,0:T(8,128)(2,1)S(1)}, bf16[288,256]{1,0:T(8,128)(2,1)S(1)}, u32[]{:S(2)}, u32[]{:S(2)}) collective-permute-start(bf16[288,256]{1,0:T(8,128)(2,1)S(1)} %concatenate.18.up0), channel_id=1, source_target_pairs={{0,6},{2,4},{4,2},{6,0},{1,7},{3,5},{5,3},{7,1},{8,14},{10,12},{12... | collective-permute-start | bytes 442376 | tf_op jit(solution)/shard_map/ppermute | solution.py:33
  21.4 0.8 %collective-permute-start.2 = (bf16[288,256]{1,0:T(8,128)(2,1)S(1)}, bf16[288,256]{1,0:T(8,128)(2,1)S(1)}, u32[]{:S(2)}, u32[]{:S(2)}) collective-permute-start(bf16[288,256]{1,0:T(8,128)(2,1)S(1)} %concatenate.18.up0), channel_id=1, source_target_pairs={{0,4},{2,6},{4,0},{6,2},{1,5},{3,7},{5,1},{7,3},{8,12},{10,14},{12... | collective-permute-start | bytes 442376 | tf_op jit(solution)/shard_map/ppermute | solution.py:33
  22.2 0.5 %collective-permute-start.1 = (bf16[288,256]{1,0:T(8,128)(2,1)S(1)}, bf16[288,256]{1,0:T(8,128)(2,1)S(1)}, u32[]{:S(2)}, u32[]{:S(2)}) collective-permute-start(bf16[288,256]{1,0:T(8,128)(2,1)S(1)} %concatenate.18.up0), channel_id=1, source_target_pairs={{0,2},{2,0},{4,6},{6,4},{1,3},{3,1},{5,7},{7,5},{8,10},{10,8},{12,... | collective-permute-start | bytes 442376 | tf_op jit(solution)/shard_map/ppermute | solution.py:33
  22.8 8.8 %all-to-all-done = bf16[8,130,2,128]{3,2,1,0:T(2,128)(2,1)S(1)} async-done(((bf16[8,130,2,128]{3,2,1,0:T(2,128)(2,1)}), bf16[8,130,2,128]{3,2,1,0:T(2,128)(2,1)S(1)}, u32[]{:S(2)}, u32[]{:S(2)}) %all-to-all-start) | async-done | bytes 532512 | tf_op jit(solution)/shard_map/all_to_all | solution.py:204
  31.6 0.1 reshape.64
  31.7 0.1 pad_maximum_fusion.1
  31.8 0.6 %broadcast_in_dim.5 = f32[8,4,128]{2,1,0:T(4,128)} broadcast(f32[4,128]{1,0:T(4,128)S(1)} %pad_maximum_fusion.1), dimensions={1,2} | broadcast | bytes 18432 | tf_op jit(solution)/shard_map/broadcast_in_dim | solution.py:209
  32.4 4.3 %all-to-all-start.1 = ((f32[8,4,128]{2,1,0:T(4,128)}), f32[8,4,128]{2,1,0:T(4,128)S(1)}, u32[]{:S(2)}, u32[]{:S(2)}) async-start(f32[8,4,128]{2,1,0:T(4,128)} %broadcast_in_dim.5), calls=%async_computation.1 | async-start | bytes 32768 | tf_op jit(solution)/shard_map/all_to_all | solution.py:209
  36.7 0.1 pad_add_fusion.info
  36.8 0.1 copy.9
  36.9 0.1 copy.10.cached
  37.0 0.0 collective-permute-done.3.up3
  37.0 0.0 collective-permute-done.2.up2
  37.0 0.0 collective-permute-done.1.up1
  37.0 5.1 %all-to-all-done.1.lows = f32[8,4,128]{2,1,0:T(4,128)S(1)} async-done(((f32[8,4,128]{2,1,0:T(4,128)}), f32[8,4,128]{2,1,0:T(4,128)S(1)}, u32[]{:S(2)}, u32[]{:S(2)}) %all-to-all-start.1) | async-done | bytes 16416 | tf_op jit(solution)/shard_map/all_to_all | solution.py:209
  42.1 0.0 copy-done
  42.1 1.6 %attend.1 = f32[8,16,128]{2,1,0:T(8,128)S(1)} custom-call(s32[3]{0:T(128)S(1)} %pad_add_fusion.info, f32[8,4,128]{2,1,0:T(4,128)S(1)} %all-to-all-done.1.lows, bf16[288,256]{1,0:T(8,128)(2,1)S(1)} %concatenate.18.up0, bf16[288,256]{1,0:T(8,128)(2,1)S(1)} %collective-permute-done.1.up1, bf16[288,256]{1,0:T(8,128)(2,1)S(1)} %collective-permute-done.2.up2, ...), custom_call_target="tpu_custom_call" | custom-call | tf_op jit(solution)/shard_map/attend/pallas_call | solution.py:231
  43.7 8.0 %all_to_all.15 = f32[8,16,128]{2,1,0:T(8,128)S(1)} all-to-all(f32[8,16,128]{2,1,0:T(8,128)S(1)} %attend.1), channel_id=1, replica_groups=mesh['role'=2,'grp'=4,'y'=4,'x'=4,'core'=2] {'x','core'}, dimensions={0} | all-to-all | bytes 131072 | tf_op jit(solution)/shard_map/all_to_all | solution.py:240
  51.7 0.1 slice_reduce_fusion
  51.8 0.2 fusion
  52.0 0.1 div.11
  52.1 0.1 fusion.1
  52.2 0.7 %fusion.6 = bf16[4,1,256]{2,0,1:T(4,128)(2,1)} fusion(f32[2,4,128]{2,1,0:T(4,128)S(1)} %bitcast.36, f32[2,4]{1,0:T(2,128)S(1)} %div.11), kind=kLoop, calls=%fused_computation.25 | loop fusion | flops 2048 | bytes 6176 | tf_op jit(solution)/shard_map/convert_element_type | solution.py:171
  (7 shorter events, 0.1 us)
Async XLA Ops:
  0.0 17.2 %copy-start.1 = (bf16[2,1,64,256]{3,2,1,0:T(8,128)(2,1)S(1)}, bf16[2,1,64,256]{3,2,1,0:T(8,128)(2,1)}, u32[]{:S(2)}) copy-start(bf16[2,1,64,256]{3,2,1,0:T(8,128)(2,1)} %param.10) | copy-start | bytes 196612
  0.0 42.1 %copy-start = (bf16[4,1,2,1024]{3,2,1,0:T(2,128)(2,1)S(1)}, bf16[4,1,2,1024]{3,2,1,0:T(2,128)(2,1)}, u32[]{:S(2)}) copy-start(bf16[4,1,2,1024]{3,2,1,0:T(2,128)(2,1)} %newest.1) | copy-start | bytes 49156
  2.3 29.3 %all-to-all-start = ((bf16[8,130,2,128]{3,2,1,0:T(2,128)(2,1)}), bf16[8,130,2,128]{3,2,1,0:T(2,128)(2,1)S(1)}, u32[]{:S(2)}, u32[]{:S(2)}) async-start(bf16[8,130,2,128]{3,2,1,0:T(2,128)(2,1)} %split.1), calls=%async_computation | async-start | bytes 1064960 | tf_op jit(solution)/shard_map/all_to_all | solution.py:204
  17.2 1.3 %collective-permute-start = (bf16[144,256]{1,0:T(8,128)(2,1)S(1)}, bf16[144,256]{1,0:T(8,128)(2,1)S(1)}, u32[]{:S(2)}, u32[]{:S(2)}) collective-permute-start(bf16[144,256]{1,0:T(8,128)(2,1)S(1)} %concatenate.17), channel_id=1, source_target_pairs={{0,1},{1,0},{2,3},{3,2},{4,5},{5,4},{6,7},{7,6},{8,9},{9,8},{10,11... | collective-permute-start | bytes 221192 | tf_op jit(solution)/shard_map/ppermute | solution.py:33
  18.6 18.4 %collective-permute-start.3 = (bf16[288,256]{1,0:T(8,128)(2,1)S(1)}, bf16[288,256]{1,0:T(8,128)(2,1)S(1)}, u32[]{:S(2)}, u32[]{:S(2)}) collective-permute-start(bf16[288,256]{1,0:T(8,128)(2,1)S(1)} %concatenate.18.up0), channel_id=1, source_target_pairs={{0,6},{2,4},{4,2},{6,0},{1,7},{3,5},{5,3},{7,1},{8,14},{10,12},{12... | collective-permute-start | bytes 442376 | tf_op jit(solution)/shard_map/ppermute | solution.py:33
  21.4 15.5 %collective-permute-start.2 = (bf16[288,256]{1,0:T(8,128)(2,1)S(1)}, bf16[288,256]{1,0:T(8,128)(2,1)S(1)}, u32[]{:S(2)}, u32[]{:S(2)}) collective-permute-start(bf16[288,256]{1,0:T(8,128)(2,1)S(1)} %concatenate.18.up0), channel_id=1, source_target_pairs={{0,4},{2,6},{4,0},{6,2},{1,5},{3,7},{5,1},{7,3},{8,12},{10,14},{12... | collective-permute-start | bytes 442376 | tf_op jit(solution)/shard_map/ppermute | solution.py:33
  22.2 14.7 %collective-permute-start.1 = (bf16[288,256]{1,0:T(8,128)(2,1)S(1)}, bf16[288,256]{1,0:T(8,128)(2,1)S(1)}, u32[]{:S(2)}, u32[]{:S(2)}) collective-permute-start(bf16[288,256]{1,0:T(8,128)(2,1)S(1)} %concatenate.18.up0), channel_id=1, source_target_pairs={{0,2},{2,0},{4,6},{6,4},{1,3},{3,1},{5,7},{7,5},{8,10},{10,8},{12,... | collective-permute-start | bytes 442376 | tf_op jit(solution)/shard_map/ppermute | solution.py:33
  32.4 9.7 %all-to-all-start.1 = ((f32[8,4,128]{2,1,0:T(4,128)}), f32[8,4,128]{2,1,0:T(4,128)S(1)}, u32[]{:S(2)}, u32[]{:S(2)}) async-start(f32[8,4,128]{2,1,0:T(4,128)} %broadcast_in_dim.5), calls=%async_computation.1 | async-start | bytes 32768 | tf_op jit(solution)/shard_map/all_to_all | solution.py:209

commit v4 on v3

--- a/solution.py
+++ b/solution.py
@@ -154,21 +154,30 @@
         summed = summed + jnp.dot(
             weight.astype(jnp.bfloat16), values, preferred_element_type=jnp.float32
         )
-    stats = jnp.where(lane < 64, top, total)
+    top = jnp.broadcast_to(top, summed.shape)
+    total = jnp.broadcast_to(total, summed.shape)
     each = 2 * DECODE_STEPS
     for d in range(BLOCK):
-        out[place ^ d, :each, :] = summed[d * each : (d + 1) * each, :]
-        out[place ^ d, each:, :] = stats[d * each : (d + 1) * each, :]
+        rows = slice(d * each, (d + 1) * each)
+        for i, value in enumerate((summed, top, total)):
+            out[place ^ d, i * each : (i + 1) * each, :] = value[rows, :]
 
 
 def combine(parts):
     each = 2 * DECODE_STEPS
-    summed, stats = parts[:, :each], parts[:, each:]
-    tops, totals = stats[:, :, :1], stats[:, :, 64:65]
-    factor = jnp.exp(tops - jnp.max(tops, axis=0, keepdims=True))
-    whole = jnp.sum(summed * factor, axis=0) / jnp.sum(totals * factor, axis=0)
-    whole = whole.reshape(2, DECODE_STEPS, HEAD_WIDTH).swapaxes(0, 1)
-    return whole.reshape(DECODE_STEPS, 2 * HEAD_WIDTH).astype(jnp.bfloat16)
+    summed, tops, totals = (
+        [parts[d, i * each : (i + 1) * each] for d in range(BLOCK)] for i in range(3)
+    )
+    top = tops[0]
+    for other in tops[1:]:
+        top = jnp.maximum(top, other)
+    above, below = 0.0, 0.0
+    for d in range(BLOCK):
+        factor = jnp.exp(tops[d] - top)
+        above = above + summed[d] * factor
+        below = below + totals[d] * factor
+    whole = (above / below).astype(jnp.bfloat16)
+    return jnp.concatenate([whole[:DECODE_STEPS], whole[DECODE_STEPS:]], axis=1)
 
 
 def local(hidden, current_weight, down_factors, up_factors, cache, step_key_value, lengths):
@@ -230,7 +239,7 @@
 
     parts = pl.pallas_call(
         attend_kernel,
-        out_shape=jax.ShapeDtypeStruct((BLOCK, 4 * DECODE_STEPS, HEAD_WIDTH), jnp.float32),
+        out_shape=jax.ShapeDtypeStruct((BLOCK, 6 * DECODE_STEPS, HEAD_WIDTH), jnp.float32),
         in_specs=[smem] + [vmem] * 8,
         out_specs=vmem,
         scratch_shapes=[pltpu.VMEM((ROWS, HEAD_WIDTH), jnp.float32)],

time: 53.2 us -> 52.8 us (level)
    convert_element_type x1, other arithmetic: 0.67 us -> 0.03 us  [combine(): whole = (above / below).astype(jnp.bfloat16)]
    broadcast_in_dim x0 -> x1, other arithmetic: none -> 0.59 us  [local(): return out[:, None, :]]
where the time goes in v4:
time: 52.8 us; the launch traced here: 52.5 us
  starting transfers between devices  18.8 us (36%)
  waiting for transfers between devices  14.2 us (27%)
  blocking collectives  8.18 us (15%)
  matrix products  4.65 us (9%)
  Pallas kernels  3.9 us (7%)
  other arithmetic  1.03 us (2%)
  local copies, waits for them, and re-layouts  0.99 us (2%)
  between operations  0.78 us (1%)
    all_to_all x1, starting transfers between devices, local(): cached = lax.all_to_all(sent, ('role', 'y'), 0, 0)  10.2 us
    all_to_all x1, waiting for transfers between devices, local(): cached = lax.all_to_all(sent, ('role', 'y'), 0, 0)  8.78 us
    all_to_all x1, blocking collectives, local(): parts = lax.all_to_all(parts, block, 0, 0)  8.18 us
    all_to_all x1, waiting for transfers between devices, local(): lax.all_to_all(jnp.broadcast_to(low, (BLOCK,) + low.shape), block, 0, 0)  5.08 us
    dot_general x1, matrix products, local(): base = jnp.dot(rows, current_weight, preferred_element_type=jnp.float32)  4.65 us
    all_to_all x1, starting transfers between devices, local(): lax.all_to_all(jnp.broadcast_to(low, (BLOCK,) + low.shape), block, 0, 0)  4.3 us
    ppermute x4, starting transfers between devices, swapped(): return lax.ppermute(block, axis, [(i, i ^ apart) for i in range(count)])  4.25 us
    pallas_call x1, Pallas kernels, local(): pl.pallas_call(split_kernel, out_shape=sent, in_specs=[smem] + [hbm] * 3,...  2.26 us
  transfers between devices with their start and end apart: 6, of which 3 were waited for; matrix products, arithmetic and copies ran while one was open for 11% of the time, Pallas kernels for 0%

profile of v4, /device:TPU:32, one launch (start us, length us, event | category | flops | bytes accessed | tf_op | source)
XLA Modules:
  0.0 52.5 jit_solution(13500197851902071501)
XLA Ops:
  0.0 0.0 copy-start.1
  0.0 0.0 copy-start
  0.0 2.3 %split.1 = bf16[8,130,2,128]{3,2,1,0:T(2,128)(2,1)} custom-call(s32[1]{0:T(128)} %bitcast.2.info, bf16[4,16384]{1,0:T(4,128)(2,1)} %bitcast.186, bf16[64,512]{1,0:T(8,128)(2,1)} %bitcast.190, bf16[128,2,1024]{2,1,0:T(2,128)(2,1)} %bitcast.187), custom_call_target="tpu_custom_call" | custom-call | tf_op jit(solution)/shard_map/split/pallas_call | solution.py:198
  2.3 10.2 %all-to-all-start = ((bf16[8,130,2,128]{3,2,1,0:T(2,128)(2,1)}), bf16[8,130,2,128]{3,2,1,0:T(2,128)(2,1)S(1)}, u32[]{:S(2)}, u32[]{:S(2)}) async-start(bf16[8,130,2,128]{3,2,1,0:T(2,128)(2,1)} %split.1), calls=%async_computation | async-start | bytes 1064960 | tf_op jit(solution)/shard_map/all_to_all | solution.py:213
  12.5 4.6 %fusion.1 = (bf16[4,256]{1,0:T(4,128)(2,1)S(1)}, bf16[4,256]{1,0:T(4,128)(2,1)S(1)}, bf16[4,256]{1,0:T(4,128)(2,1)S(1)}) fusion(bf16[16384,256]{1,0:T(8,128)(2,1)} %param.8, bf16[4,1,16384]{2,0,1:T(4,128)(2,1)} %param.7), kind=kOutput, calls=%fused_computation.7 | convolution fusion | flops 33561600 | bytes 8525824 | tf_op jit(solution)/shard_map/dot_general | solution.py:221
  17.2 0.0 copy-done.1
  17.2 0.1 concatenate.20
  17.2 0.1 collective-permute-start
  18.0 0.1 multiply_cosine_fusion
  18.1 0.1 maximum_bitcast_fusion
  18.2 0.4 collective-permute-done
  18.6 0.1 concatenate.21.up0
  18.6 2.8 %collective-permute-start.3 = (bf16[288,256]{1,0:T(8,128)(2,1)S(1)}, bf16[288,256]{1,0:T(8,128)(2,1)S(1)}, u32[]{:S(2)}, u32[]{:S(2)}) collective-permute-start(bf16[288,256]{1,0:T(8,128)(2,1)S(1)} %concatenate.21.up0), channel_id=1, source_target_pairs={{0,6},{2,4},{4,2},{6,0},{1,7},{3,5},{5,3},{7,1},{8,14},{10,12},{12... | collective-permute-start | bytes 442376 | tf_op jit(solution)/shard_map/ppermute | solution.py:33
  21.4 0.8 %collective-permute-start.2 = (bf16[288,256]{1,0:T(8,128)(2,1)S(1)}, bf16[288,256]{1,0:T(8,128)(2,1)S(1)}, u32[]{:S(2)}, u32[]{:S(2)}) collective-permute-start(bf16[288,256]{1,0:T(8,128)(2,1)S(1)} %concatenate.21.up0), channel_id=1, source_target_pairs={{0,4},{2,6},{4,0},{6,2},{1,5},{3,7},{5,1},{7,3},{8,12},{10,14},{12... | collective-permute-start | bytes 442376 | tf_op jit(solution)/shard_map/ppermute | solution.py:33
  22.2 0.5 %collective-permute-start.1 = (bf16[288,256]{1,0:T(8,128)(2,1)S(1)}, bf16[288,256]{1,0:T(8,128)(2,1)S(1)}, u32[]{:S(2)}, u32[]{:S(2)}) collective-permute-start(bf16[288,256]{1,0:T(8,128)(2,1)S(1)} %concatenate.21.up0), channel_id=1, source_target_pairs={{0,2},{2,0},{4,6},{6,4},{1,3},{3,1},{5,7},{7,5},{8,10},{10,8},{12,... | collective-permute-start | bytes 442376 | tf_op jit(solution)/shard_map/ppermute | solution.py:33
  22.8 8.8 %all-to-all-done = bf16[8,130,2,128]{3,2,1,0:T(2,128)(2,1)S(1)} async-done(((bf16[8,130,2,128]{3,2,1,0:T(2,128)(2,1)}), bf16[8,130,2,128]{3,2,1,0:T(2,128)(2,1)S(1)}, u32[]{:S(2)}, u32[]{:S(2)}) %all-to-all-start) | async-done | bytes 532512 | tf_op jit(solution)/shard_map/all_to_all | solution.py:213
  31.6 0.1 reshape.38
  31.7 0.1 pad_maximum_fusion.1
  31.8 0.6 %broadcast_in_dim.14 = f32[8,4,128]{2,1,0:T(4,128)} broadcast(f32[4,128]{1,0:T(4,128)S(1)} %pad_maximum_fusion.1), dimensions={1,2} | broadcast | bytes 18432 | tf_op jit(solution)/shard_map/broadcast_in_dim | solution.py:218
  32.4 4.3 %all-to-all-start.1 = ((f32[8,4,128]{2,1,0:T(4,128)}), f32[8,4,128]{2,1,0:T(4,128)S(1)}, u32[]{:S(2)}, u32[]{:S(2)}) async-start(f32[8,4,128]{2,1,0:T(4,128)} %broadcast_in_dim.14), calls=%async_computation.1 | async-start | bytes 32768 | tf_op jit(solution)/shard_map/all_to_all | solution.py:218
  36.7 0.1 pad_add_fusion.info
  36.8 0.1 copy.8
  36.9 0.1 copy.9.cached
  37.0 0.0 collective-permute-done.3.up3
  37.0 0.0 collective-permute-done.2.up2
  37.0 0.0 collective-permute-done.1.up1
  37.0 5.1 %all-to-all-done.1.lows = f32[8,4,128]{2,1,0:T(4,128)S(1)} async-done(((f32[8,4,128]{2,1,0:T(4,128)}), f32[8,4,128]{2,1,0:T(4,128)S(1)}, u32[]{:S(2)}, u32[]{:S(2)}) %all-to-all-start.1) | async-done | bytes 16416 | tf_op jit(solution)/shard_map/all_to_all | solution.py:218
  42.1 0.0 copy-done
  42.1 1.6 %attend.1 = f32[8,24,128]{2,1,0:T(8,128)S(1)} custom-call(s32[3]{0:T(128)S(1)} %pad_add_fusion.info, f32[8,4,128]{2,1,0:T(4,128)S(1)} %all-to-all-done.1.lows, bf16[288,256]{1,0:T(8,128)(2,1)S(1)} %concatenate.21.up0, bf16[288,256]{1,0:T(8,128)(2,1)S(1)} %collective-permute-done.1.up1, bf16[288,256]{1,0:T(8,128)(2,1)S(1)} %collective-permute-done.2.up2, ...), custom_call_target="tpu_custom_call" | custom-call | tf_op jit(solution)/shard_map/attend/pallas_call | solution.py:240
  43.7 8.2 %all_to_all.15 = f32[8,24,128]{2,1,0:T(8,128)S(1)} all-to-all(f32[8,24,128]{2,1,0:T(8,128)S(1)} %attend.1), channel_id=1, replica_groups=mesh['role'=2,'grp'=4,'y'=4,'x'=4,'core'=2] {'x','core'}, dimensions={0} | all-to-all | bytes 196608 | tf_op jit(solution)/shard_map/all_to_all | solution.py:249
  51.9 0.6 %maximum_bitcast_fusion.2 = bf16[4,1,256]{2,0,1:T(4,128)(2,1)} fusion(bf16[4,128]{1,0:T(4,128)(2,1)S(1)} %get-tuple-element.11, bf16[4,128]{1,0:T(4,128)(2,1)S(1)} %get-tuple-element.10), kind=kLoop, calls=%fused_computation.73 | loop fusion | flops 4096 | bytes 4096 | tf_op jit(solution)/shard_map/broadcast_in_dim | solution.py:251
  (9 shorter events, 0.1 us)
Async XLA Ops:
  0.0 17.2 %copy-start.1 = (bf16[2,1,64,256]{3,2,1,0:T(8,128)(2,1)S(1)}, bf16[2,1,64,256]{3,2,1,0:T(8,128)(2,1)}, u32[]{:S(2)}) copy-start(bf16[2,1,64,256]{3,2,1,0:T(8,128)(2,1)} %param.10) | copy-start | bytes 196612
  0.0 42.1 %copy-start = (bf16[4,1,2,1024]{3,2,1,0:T(2,128)(2,1)S(1)}, bf16[4,1,2,1024]{3,2,1,0:T(2,128)(2,1)}, u32[]{:S(2)}) copy-start(bf16[4,1,2,1024]{3,2,1,0:T(2,128)(2,1)} %newest.1) | copy-start | bytes 49156
  2.3 29.3 %all-to-all-start = ((bf16[8,130,2,128]{3,2,1,0:T(2,128)(2,1)}), bf16[8,130,2,128]{3,2,1,0:T(2,128)(2,1)S(1)}, u32[]{:S(2)}, u32[]{:S(2)}) async-start(bf16[8,130,2,128]{3,2,1,0:T(2,128)(2,1)} %split.1), calls=%async_computation | async-start | bytes 1064960 | tf_op jit(solution)/shard_map/all_to_all | solution.py:213
  17.2 1.3 %collective-permute-start = (bf16[144,256]{1,0:T(8,128)(2,1)S(1)}, bf16[144,256]{1,0:T(8,128)(2,1)S(1)}, u32[]{:S(2)}, u32[]{:S(2)}) collective-permute-start(bf16[144,256]{1,0:T(8,128)(2,1)S(1)} %concatenate.20), channel_id=1, source_target_pairs={{0,1},{1,0},{2,3},{3,2},{4,5},{5,4},{6,7},{7,6},{8,9},{9,8},{10,11... | collective-permute-start | bytes 221192 | tf_op jit(solution)/shard_map/ppermute | solution.py:33
  18.6 18.4 %collective-permute-start.3 = (bf16[288,256]{1,0:T(8,128)(2,1)S(1)}, bf16[288,256]{1,0:T(8,128)(2,1)S(1)}, u32[]{:S(2)}, u32[]{:S(2)}) collective-permute-start(bf16[288,256]{1,0:T(8,128)(2,1)S(1)} %concatenate.21.up0), channel_id=1, source_target_pairs={{0,6},{2,4},{4,2},{6,0},{1,7},{3,5},{5,3},{7,1},{8,14},{10,12},{12... | collective-permute-start | bytes 442376 | tf_op jit(solution)/shard_map/ppermute | solution.py:33
  21.4 15.5 %collective-permute-start.2 = (bf16[288,256]{1,0:T(8,128)(2,1)S(1)}, bf16[288,256]{1,0:T(8,128)(2,1)S(1)}, u32[]{:S(2)}, u32[]{:S(2)}) collective-permute-start(bf16[288,256]{1,0:T(8,128)(2,1)S(1)} %concatenate.21.up0), channel_id=1, source_target_pairs={{0,4},{2,6},{4,0},{6,2},{1,5},{3,7},{5,1},{7,3},{8,12},{10,14},{12... | collective-permute-start | bytes 442376 | tf_op jit(solution)/shard_map/ppermute | solution.py:33
  22.2 14.7 %collective-permute-start.1 = (bf16[288,256]{1,0:T(8,128)(2,1)S(1)}, bf16[288,256]{1,0:T(8,128)(2,1)S(1)}, u32[]{:S(2)}, u32[]{:S(2)}) collective-permute-start(bf16[288,256]{1,0:T(8,128)(2,1)S(1)} %concatenate.21.up0), channel_id=1, source_target_pairs={{0,2},{2,0},{4,6},{6,4},{1,3},{3,1},{5,7},{7,5},{8,10},{10,8},{12,... | collective-permute-start | bytes 442376 | tf_op jit(solution)/shard_map/ppermute | solution.py:33
  32.4 9.7 %all-to-all-start.1 = ((f32[8,4,128]{2,1,0:T(4,128)}), f32[8,4,128]{2,1,0:T(4,128)S(1)}, u32[]{:S(2)}, u32[]{:S(2)}) async-start(f32[8,4,128]{2,1,0:T(4,128)} %broadcast_in_dim.14), calls=%async_computation.1 | async-start | bytes 32768 | tf_op jit(solution)/shard_map/all_to_all | solution.py:218

commit v5 on v2

v5 whole, which is shorter than its diff:
```python
import math

import jax
import jax.numpy as jnp
from jax import lax
from jax.experimental import pallas as pl
from jax.experimental.pallas import tpu as pltpu
from jax.sharding import Mesh, PartitionSpec as P

QUERY_HEADS = 128
KEY_VALUE_HEADS = 8
HEAD_WIDTH = 128
DECODE_STEPS = 4
BLOCK_X = 4
BLOCK_CORE = 2
BLOCK = BLOCK_X * BLOCK_CORE
SHARE = QUERY_HEADS // KEY_VALUE_HEADS
ROWS = SHARE * DECODE_STEPS
MASKED = -1e30


def angles(pos):
    half = HEAD_WIDTH // 2
    freq = jnp.exp(
        jnp.arange(half, dtype=jnp.float32) * (-2.0 * math.log(500000.0) / HEAD_WIDTH)
    )
    angle = pos.astype(jnp.float32)[:, None] * freq
    return jnp.cos(angle), jnp.sin(angle)


def swapped(block, axis, apart):
    count = lax.axis_size(axis)
    return lax.ppermute(block, axis, [(i, i ^ apart) for i in range(count)])


def split_kernel(info, hidden, down, cache, out):
    depth = down.shape[1]
    own = pl.ds(pl.multiple_of(info[0] * depth, depth), depth)
    part = lax.dot_general(
        hidden[:, own], down[...], (((1,), (1,)), ((), ())), preferred_element_type=jnp.float32
    )
    high = part.astype(jnp.bfloat16).astype(jnp.float32)
    terms = jnp.concatenate([high, part - high], axis=1).astype(jnp.bfloat16)
    share = cache.shape[0] // BLOCK
    for head in range(KEY_VALUE_HEADS):
        columns = slice(head * HEAD_WIDTH, (head + 1) * HEAD_WIDTH)
        for d in range(BLOCK):
            to = head * BLOCK + d
            out[to, :share] = cache[d * share : (d + 1) * share, :, columns]
            for t in range(DECODE_STEPS):
                out[to, share + t // 2, t % 2, :] = terms[t]


def attend_kernel(
    info, pos, pick, up0, up1, up2, up3, turn, cached, newest, out, query
):
    ups = (up0, up1, up2, up3)
    length = info[0]
    place = info[1]
    sums = jnp.dot(pick[...], cached[...], preferred_element_type=jnp.float32)
    half = HEAD_WIDTH // 2
    low = [
        sums[i * DECODE_STEPS : (i + 1) * DECODE_STEPS, :half]
        + sums[i * DECODE_STEPS : (i + 1) * DECODE_STEPS, half:]
        for i in range(2)
    ]
    low = jnp.concatenate(low, axis=1)
    rank = low.shape[1]
    high = low.astype(jnp.bfloat16).astype(jnp.float32)
    rest = low - high
    middle = rest.astype(jnp.bfloat16).astype(jnp.float32)
    terms = jnp.concatenate([high, middle, rest - middle, jnp.zeros_like(low)], axis=0).astype(
        jnp.bfloat16
    )
    cosine = turn[0]
    sine = turn[1]
    for j in range(BLOCK):
        step = up0.shape[0] // BLOCK_CORE
        start = pl.multiple_of((place ^ j) % BLOCK_CORE * step, 16)
        both = ups[j // BLOCK_CORE]
        extra = jnp.dot(
            terms, both[pl.ds(start, rank), :], preferred_element_type=jnp.float32
        )
        base = both[pl.ds(start + rank, 16), :].astype(jnp.float32)
        raw = ((base[8:12] + base[4:8]) + base[0:4]) + ((extra[8:12] + extra[4:8]) + extra[0:4])
        for i in range(2):
            head = raw[:, i * HEAD_WIDTH : (i + 1) * HEAD_WIDTH]
            row = (2 * j + i) * DECODE_STEPS
            query[row : row + DECODE_STEPS, :] = head * cosine + pltpu.roll(head, 64, 1) * sine
    queries = query[...].astype(jnp.bfloat16)
    scale = 1.0 / math.sqrt(HEAD_WIDTH)
    own = pl.ds(pl.multiple_of(info[2] * HEAD_WIDTH, HEAD_WIDTH), HEAD_WIDTH)
    token = newest[:, 0, 0, own].astype(jnp.float32)
    token = token * cosine + pltpu.roll(token, 64, 1) * sine
    blank = jnp.zeros((HEAD_WIDTH - DECODE_STEPS, HEAD_WIDTH), jnp.float32)
    fresh_key = jnp.concatenate([token, blank], axis=0).astype(jnp.bfloat16)
    fresh_value = jnp.concatenate(
        [newest[:, 0, 1, own].astype(jnp.float32), blank], axis=0
    ).astype(jnp.bfloat16)
    chunk = 256
    n_src = cached.shape[0] // chunk
    blocks = [slice(j * chunk, (j + 1) * chunk) for j in range(n_src)]
    row = lax.broadcasted_iota(jnp.int32, (ROWS, HEAD_WIDTH), 0)
    lane = lax.broadcasted_iota(jnp.int32, (ROWS, HEAD_WIDTH), 1)
    contract = (((1,), (1,)), ((), ()))
    masks = []
    scores = []
    for j in range(n_src):
        keys = cached[blocks[j], :]
        s = lax.dot_general(queries, keys, contract, preferred_element_type=jnp.float32)
        ok = jnp.broadcast_to(pos[:, blocks[j]] < length, s.shape)
        masks.append(ok)
        scores.append(jnp.where(ok, s * scale, MASKED))
    s = lax.dot_general(queries, fresh_key, contract, preferred_element_type=jnp.float32)
    ok = (lane <= lax.rem(row, DECODE_STEPS)) & (place == 0)
    masks.append(ok)
    scores.append(jnp.where(ok, s * scale, MASKED))
    top = jnp.max(scores[-1], axis=-1, keepdims=True)
    for s in scores[:-1]:
        top = jnp.maximum(top, jnp.max(s, axis=-1, keepdims=True))
    total = jnp.zeros_like(top)
    summed = jnp.zeros((ROWS, HEAD_WIDTH), jnp.float32)
    for j in range(n_src + 1):
        weight = jnp.where(masks[j], jnp.exp(scores[j] - top), 0.0)
        total = total + jnp.sum(weight, axis=-1, keepdims=True)
        if j < n_src:
            weight, values = pltpu.roll(weight, 1, 1), cached[blocks[j], :]
        else:
            values = fresh_value
        summed = summed + jnp.dot(
            weight.astype(jnp.bfloat16), values, preferred_element_type=jnp.float32
        )
    top = jnp.broadcast_to(top, summed.shape)
    total = jnp.broadcast_to(total, summed.shape)
    each = 2 * DECODE_STEPS
    for d in range(BLOCK):
        rows = slice(d * each, (d + 1) * each)
        for i, value in enumerate((summed, top, total)):
            out[place ^ d, i * each : (i + 1) * each, :] = value[rows, :]


def combine(parts):
    each = 2 * DECODE_STEPS
    summed, tops, totals = (
        [parts[d, i * each : (i + 1) * each] for d in range(BLOCK)] for i in range(3)
    )
    top = tops[0]
    for other in tops[1:]:
        top = jnp.maximum(top, other)
    above, below = 0.0, 0.0
    for d in range(BLOCK):
        factor = jnp.exp(tops[d] - top)
        above = above + summed[d] * factor
        below = below + totals[d] * factor
    whole = (above / below).astype(jnp.bfloat16)
    return jnp.concatenate([whole[:DECODE_STEPS], whole[DECODE_STEPS:]], axis=1)


def local(hidden, current_weight, down_factors, up_factors, cache, step_key_value, lengths):
    plane = ("y", "x", "core")
    block = ("x", "core")
    shard = lax.axis_index(plane)
    place = lax.axis_index(block)
    key_head = lax.axis_index(("role", "y"))
    rows = hidden.reshape(DECODE_STEPS, -1)
    down = down_factors[0, 0].T
    vmem = pl.BlockSpec(memory_space=pltpu.VMEM)
    smem = pl.BlockSpec(memory_space=pltpu.SMEM)
    everyone = ("role",) + plane
    share = cache.shape[1] // BLOCK
    sent = pl.pallas_call(
        split_kernel,
        out_shape=jax.ShapeDtypeStruct(
            (lax.axis_size(everyone), share + DECODE_STEPS // 2, 2, HEAD_WIDTH), cache.dtype
        ),
        in_specs=[smem] + [vmem] * 3,
        out_specs=vmem,
        name="split",
    )(shard[None].astype(jnp.int32), rows, down, cache[0])
    cached = lax.all_to_all(sent, everyone, 0, 0)
    rows_each = 2 * cached.shape[1]
    cached = cached.reshape(-1, HEAD_WIDTH)
    column = jnp.arange(cached.shape[0], dtype=jnp.int32)
    source, inner = column // rows_each, column % rows_each
    pos = source * cache.shape[1] + place * share + inner // 2
    pos = jnp.where((inner < 2 * share) & (inner % 2 == 0), pos, jnp.int32(2**30))[None]
    step = jnp.arange(16, dtype=jnp.int32)[:, None]
    new = source < lax.axis_size(everyone) // 2
    wanted = (inner >= 2 * share) & (inner - 2 * share == step % DECODE_STEPS)
    wanted = wanted & (step // DECODE_STEPS == jnp.where(new, 0, 1))
    pick = jnp.where(wanted, jnp.where(new, 1.0, -1.0), 0.0).astype(jnp.bfloat16)

    rows, sent = lax.optimization_barrier((rows, sent))
    base = jnp.dot(rows, current_weight, preferred_element_type=jnp.float32)
    high = lax.reduce_precision(base, 8, 7)
    middle = lax.reduce_precision(base - high, 8, 7)
    parts = [high, middle, base - high - middle, jnp.zeros_like(base)]
    parts = [term.astype(jnp.bfloat16) for term in parts]
    up = jnp.concatenate([up_factors.reshape(-1, up_factors.shape[-1])] + parts, axis=0)
    up = lax.all_gather(up, "core", axis=0, tiled=True)
    ups = [up] + [swapped(up, "x", m) for m in range(1, BLOCK_X)]

    steps_pos = lengths[None, :] + jnp.arange(DECODE_STEPS, dtype=jnp.int32)[:, None]
    cosine, sine = angles(steps_pos[:, 0])
    turn = jnp.stack(
        [
            jnp.concatenate([cosine, cosine], axis=-1),
            jnp.concatenate([-sine, sine], axis=-1),
        ]
    )
    info = jnp.stack([lengths[0], place, key_head]).astype(jnp.int32)

    parts = pl.pallas_call(
        attend_kernel,
        out_shape=jax.ShapeDtypeStruct((BLOCK, 6 * DECODE_STEPS, HEAD_WIDTH), jnp.float32),
        in_specs=[smem] + [vmem] * 9,
        out_specs=vmem,
        scratch_shapes=[pltpu.VMEM((ROWS, HEAD_WIDTH), jnp.float32)],
        compiler_params=pltpu.CompilerParams(vmem_limit_bytes=16 * 2**20),
        name="attend",
    )(info, pos, pick, *ups, turn, cached, step_key_value)
    parts = lax.all_to_all(parts, block, 0, 0)
    out = combine(parts)
    return out[:, None, :]


def solution(mesh):
    role, grp, tp = mesh.devices.shape
    finer = Mesh(
        mesh.devices.reshape(role, grp, tp // BLOCK, BLOCK_X, BLOCK_CORE),
        ("role", "grp", "y", "x", "core"),
    )
    tp = ("y", "x", "core")
    both = ("role",) + tp
    placed = (
        P(None, "grp", None),
        P(None, both),
        P("role", "grp", tp, None),
        P(None, "grp", None, both),
        P("grp", both, None, None),
        P(None, "grp", None, None),
        P("grp"),
    )
    return jax.shard_map(
        local, mesh=finer, in_specs=placed, out_specs=P(None, "grp", both), check_vma=False
    )
```

time: 53.6 us -> 50.7 us (0.946)
  waiting for transfers between devices: 14.3 us -> 10.6 us
  blocking collectives: 8 us -> 10.9 us
  starting transfers between devices: 19.3 us -> 17.8 us
  local copies, waits for them, and re-layouts: 0.72 us -> 0.07 us
    all_to_all x2 -> x1, waiting for transfers between devices: 14.3 us -> 2.35 us  [local(): cached = lax.all_to_all(sent, everyone, 0, 0)]
    ppermute x4 -> x3, waiting for transfers between devices: 0.01 us -> 8.27 us  [swapped(): return lax.ppermute(block, axis, [(i, i ^ apart) for i in range(count)])]
    all_gather x0 -> x1, blocking collectives: none -> 1.9 us  [local(): up = lax.all_gather(up, 'core', axis=0, tiled=True)]
    all_to_all x1, blocking collectives: 8 us -> 8.98 us  [local(): parts = lax.all_to_all(parts, block, 0, 0)]
    all_to_all x2 -> x1, starting transfers between devices: 14.5 us -> 13.7 us  [local(): cached = lax.all_to_all(sent, everyone, 0, 0)]
    ppermute x4 -> x3, starting transfers between devices: 4.79 us -> 4.1 us  [swapped(): return lax.ppermute(block, axis, [(i, i ^ apart) for i in range(count)])]
    broadcast_in_dim x1 -> x0, local copies, waits for them, and re-layouts: 0.63 us -> none  [local(): jnp.broadcast_to(message, (BLOCK,) + message.shape)]
    broadcast_in_dim x0 -> x1, other arithmetic: none -> 0.59 us  [local(): return out[:, None, :]]
  transfers between devices with their start and end apart: 6 -> 4, of which waited for: 2 -> 4; matrix products, arithmetic and copies ran while one was open for 11% -> 10% of each run, Pallas kernels for 0% -> 0%
where the time goes in v5:
time: 50.7 us; the launch traced here: 50.4 us
  starting transfers between devices  17.8 us (35%)
  blocking collectives  10.9 us (21%)
  waiting for transfers between devices  10.6 us (21%)
  matrix products  4.65 us (9%)
  Pallas kernels  4.53 us (9%)
  other arithmetic  1.17 us (2%)
  between operations  0.74 us (1%)
    all_to_all x1, starting transfers between devices, local(): cached = lax.all_to_all(sent, everyone, 0, 0)  13.7 us
    all_to_all x1, blocking collectives, local(): parts = lax.all_to_all(parts, block, 0, 0)  8.98 us
    ppermute x3, waiting for transfers between devices, swapped(): return lax.ppermute(block, axis, [(i, i ^ apart) for i in range(count)])  8.27 us
    dot_general x1, matrix products, local(): base = jnp.dot(rows, current_weight, preferred_element_type=jnp.float32)  4.65 us
    ppermute x3, starting transfers between devices, swapped(): return lax.ppermute(block, axis, [(i, i ^ apart) for i in range(count)])  4.1 us
    pallas_call x1, Pallas kernels, local(): pl.pallas_call(split_kernel, out_shape=jax.ShapeDtypeStruct((lax.axis_siz...  2.53 us
    all_to_all x1, waiting for transfers between devices, local(): cached = lax.all_to_all(sent, everyone, 0, 0)  2.35 us
    pallas_call x1, Pallas kernels, local(): pl.pallas_call(attend_kernel, out_shape=jax.ShapeDtypeStruct((BLOCK, 6 *...  2 us
  transfers between devices with their start and end apart: 4, of which 4 were waited for; matrix products, arithmetic and copies ran while one was open for 10% of the time, Pallas kernels for 0%

profile of v5, /device:TPU:32, one launch (start us, length us, event | category | flops | bytes accessed | tf_op | source)
XLA Modules:
  0.0 50.4 jit_solution(929850543649992171)
XLA Ops:
  0.0 0.0 copy-start.1
  0.0 0.0 copy-start
  0.0 2.5 %split.1 = bf16[64,18,2,128]{3,2,1,0:T(2,128)(2,1)} custom-call(s32[1]{0:T(128)} %bitcast.4.info, bf16[4,16384]{1,0:T(4,128)(2,1)} %bitcast.179, bf16[64,512]{1,0:T(8,128)(2,1)} %bitcast.182, bf16[128,2,1024]{2,1,0:T(2,128)(2,1)} %bitcast.181), custom_call_target="tpu_custom_call" | custom-call | tf_op jit(solution)/shard_map/split/pallas_call | solution.py:171
  2.5 13.7 %all-to-all-start = ((bf16[64,18,2,128]{3,2,1,0:T(2,128)(2,1)}), bf16[64,18,2,128]{3,2,1,0:T(2,128)(2,1)S(1)}, u32[]{:S(2)}, u32[]{:S(2)}) async-start(bf16[64,18,2,128]{3,2,1,0:T(2,128)(2,1)} %split.1), calls=%async_computation | async-start | bytes 1179648 | tf_op jit(solution)/shard_map/all_to_all | solution.py:180
  16.2 4.7 %fusion.11 = (bf16[4,256]{1,0:T(4,128)(2,1)S(1)}, bf16[4,256]{1,0:T(4,128)(2,1)S(1)}, bf16[4,256]{1,0:T(4,128)(2,1)S(1)}) fusion(bf16[4,16384]{1,0:T(4,128)(2,1)} %bitcast.180, bf16[16384,256]{1,0:T(8,128)(2,1)} %param.8), kind=kOutput, calls=%fused_computation.33 | convolution fusion | flops 33561600 | bytes 8525824 | tf_op jit(solution)/shard_map/dot_general | solution.py:194
  20.9 0.0 copy-done.1
  20.9 0.1 concatenate.12
  20.9 1.9 %all_gather.3.up0 = bf16[288,256]{1,0:T(8,128)(2,1)S(1)} all-gather(bf16[144,256]{1,0:T(8,128)(2,1)S(1)} %concatenate.12), channel_id=1, replica_groups=mesh['role'=2,'grp'=4,'y'=4,'x'=4,'core'=2] {'core'}, dimensions={0}, use_global_device_ids=true | all-gather | bytes 221184 | tf_op jit(solution)/shard_map/all_gather | solution.py:200
  22.8 2.8 %collective-permute-start.2 = (bf16[288,256]{1,0:T(8,128)(2,1)S(1)}, bf16[288,256]{1,0:T(8,128)(2,1)S(1)}, u32[]{:S(2)}, u32[]{:S(2)}) collective-permute-start(bf16[288,256]{1,0:T(8,128)(2,1)S(1)} %all_gather.3.up0), channel_id=1, source_target_pairs={{0,6},{2,4},{4,2},{6,0},{1,7},{3,5},{5,3},{7,1},{8,14},{10,12},{12... | collective-permute-start | bytes 442376 | tf_op jit(solution)/shard_map/ppermute | solution.py:33
  25.6 0.9 %collective-permute-start.1 = (bf16[288,256]{1,0:T(8,128)(2,1)S(1)}, bf16[288,256]{1,0:T(8,128)(2,1)S(1)}, u32[]{:S(2)}, u32[]{:S(2)}) collective-permute-start(bf16[288,256]{1,0:T(8,128)(2,1)S(1)} %all_gather.3.up0), channel_id=1, source_target_pairs={{0,4},{2,6},{4,0},{6,2},{1,5},{3,7},{5,1},{7,3},{8,12},{10,14},{12... | collective-permute-start | bytes 442376 | tf_op jit(solution)/shard_map/ppermute | solution.py:33
  26.5 0.5 collective-permute-start
  27.7 0.1 multiply_cosine_fusion
  27.8 0.1 maximum_bitcast_fusion
  27.9 0.1 and_select_fusion.2.pos
  28.0 0.1 select_convert_fusion.pick
  28.1 0.1 pad_add_fusion.info
  28.2 6.7 %collective-permute-done.2.up3 = bf16[288,256]{1,0:T(8,128)(2,1)S(1)} collective-permute-done((bf16[288,256]{1,0:T(8,128)(2,1)S(1)}, bf16[288,256]{1,0:T(8,128)(2,1)S(1)}, u32[]{:S(2)}, u32[]{:S(2)}) %collective-permute-start.2) | collective-permute-done | bytes 147488 | tf_op jit(solution)/shard_map/ppermute | solution.py:33
  34.9 0.5 collective-permute-done.1.up2
  35.3 1.1 %collective-permute-done.up1 = bf16[288,256]{1,0:T(8,128)(2,1)S(1)} collective-permute-done((bf16[288,256]{1,0:T(8,128)(2,1)S(1)}, bf16[288,256]{1,0:T(8,128)(2,1)S(1)}, u32[]{:S(2)}, u32[]{:S(2)}) %collective-permute-start) | collective-permute-done | bytes 147488 | tf_op jit(solution)/shard_map/ppermute | solution.py:33
  36.5 2.4 %all-to-all-done = bf16[64,18,2,128]{3,2,1,0:T(2,128)(2,1)S(1)} async-done(((bf16[64,18,2,128]{3,2,1,0:T(2,128)(2,1)}), bf16[64,18,2,128]{3,2,1,0:T(2,128)(2,1)S(1)}, u32[]{:S(2)}, u32[]{:S(2)}) %all-to-all-start) | async-done | bytes 589856 | tf_op jit(solution)/shard_map/all_to_all | solution.py:180
  38.8 0.0 copy-done
  38.8 2.0 %attend.1 = f32[8,24,128]{2,1,0:T(8,128)S(1)} custom-call(s32[3]{0:T(128)S(1)} %pad_add_fusion.info, s32[1,2304]{1,0:T(1,128)S(1)} %and_select_fusion.2.pos, bf16[16,2304]{1,0:T(8,128)(2,1)S(1)} %select_convert_fusion.pick, bf16[288,256]{1,0:T(8,128)(2,1)S(1)} %all_gather.3.up0, bf16[288,256]{1,0:T(8,128)(2,1)S(1)} %collective-permute-done.up1, ...), custom_call_target="tpu_custom_call" | custom-call | tf_op jit(solution)/shard_map/attend/pallas_call | solution.py:213
  40.8 9.0 %all_to_all.10 = f32[8,24,128]{2,1,0:T(8,128)S(1)} all-to-all(f32[8,24,128]{2,1,0:T(8,128)S(1)} %attend.1), channel_id=1, replica_groups=mesh['role'=2,'grp'=4,'y'=4,'x'=4,'core'=2] {'x','core'}, dimensions={0} | all-to-all | bytes 196608 | tf_op jit(solution)/shard_map/all_to_all | solution.py:222
  49.9 0.6 %maximum_bitcast_fusion.2 = bf16[4,1,256]{2,0,1:T(4,128)(2,1)} fusion(bf16[4,128]{1,0:T(4,128)(2,1)S(1)} %get-tuple-element.11, bf16[4,128]{1,0:T(4,128)(2,1)S(1)} %get-tuple-element.10), kind=kLoop, calls=%fused_computation.95 | loop fusion | flops 4096 | bytes 4096 | tf_op jit(solution)/shard_map/broadcast_in_dim | solution.py:224
  (10 shorter events, 0.1 us)
Async XLA Ops:
  0.0 20.9 %copy-start.1 = (bf16[2,1,64,256]{3,2,1,0:T(8,128)(2,1)S(1)}, bf16[2,1,64,256]{3,2,1,0:T(8,128)(2,1)}, u32[]{:S(2)}) copy-start(bf16[2,1,64,256]{3,2,1,0:T(8,128)(2,1)} %param.10) | copy-start | bytes 196612
  0.0 38.8 %copy-start = (bf16[4,1,2,1024]{3,2,1,0:T(2,128)(2,1)S(1)}, bf16[4,1,2,1024]{3,2,1,0:T(2,128)(2,1)}, u32[]{:S(2)}) copy-start(bf16[4,1,2,1024]{3,2,1,0:T(2,128)(2,1)} %newest.1) | copy-start | bytes 49156
  2.5 36.3 %all-to-all-start = ((bf16[64,18,2,128]{3,2,1,0:T(2,128)(2,1)}), bf16[64,18,2,128]{3,2,1,0:T(2,128)(2,1)S(1)}, u32[]{:S(2)}, u32[]{:S(2)}) async-start(bf16[64,18,2,128]{3,2,1,0:T(2,128)(2,1)} %split.1), calls=%async_computation | async-start | bytes 1179648 | tf_op jit(solution)/shard_map/all_to_all | solution.py:180
  22.8 12.0 %collective-permute-start.2 = (bf16[288,256]{1,0:T(8,128)(2,1)S(1)}, bf16[288,256]{1,0:T(8,128)(2,1)S(1)}, u32[]{:S(2)}, u32[]{:S(2)}) collective-permute-start(bf16[288,256]{1,0:T(8,128)(2,1)S(1)} %all_gather.3.up0), channel_id=1, source_target_pairs={{0,6},{2,4},{4,2},{6,0},{1,7},{3,5},{5,3},{7,1},{8,14},{10,12},{12... | collective-permute-start | bytes 442376 | tf_op jit(solution)/shard_map/ppermute | solution.py:33
  25.6 9.7 %collective-permute-start.1 = (bf16[288,256]{1,0:T(8,128)(2,1)S(1)}, bf16[288,256]{1,0:T(8,128)(2,1)S(1)}, u32[]{:S(2)}, u32[]{:S(2)}) collective-permute-start(bf16[288,256]{1,0:T(8,128)(2,1)S(1)} %all_gather.3.up0), channel_id=1, source_target_pairs={{0,4},{2,6},{4,0},{6,2},{1,5},{3,7},{5,1},{7,3},{8,12},{10,14},{12... | collective-permute-start | bytes 442376 | tf_op jit(solution)/shard_map/ppermute | solution.py:33
  26.5 10.0 %collective-permute-start = (bf16[288,256]{1,0:T(8,128)(2,1)S(1)}, bf16[288,256]{1,0:T(8,128)(2,1)S(1)}, u32[]{:S(2)}, u32[]{:S(2)}) collective-permute-start(bf16[288,256]{1,0:T(8,128)(2,1)S(1)} %all_gather.3.up0), channel_id=1, source_target_pairs={{0,2},{2,0},{4,6},{6,4},{1,3},{3,1},{5,7},{7,5},{8,10},{10,8},{12,... | collective-permute-start | bytes 442376 | tf_op jit(solution)/shard_map/ppermute | solution.py:33

commit v6 on v5

--- a/solution.py
+++ b/solution.py
@@ -33,22 +33,47 @@
     return lax.ppermute(block, axis, [(i, i ^ apart) for i in range(count)])
 
 
-def split_kernel(info, hidden, down, cache, out):
+SPLITS = 4
+
+
+def split_kernel(info, hidden, down, cache, out, some, factor, held, ready, sems):
+    share = cache.shape[0] // BLOCK
+    piece = cache.shape[0] // SPLITS
     depth = down.shape[1]
     own = pl.ds(pl.multiple_of(info[0] * depth, depth), depth)
+    fetches = [
+        pltpu.make_async_copy(hidden.at[:, own], some, sems.at[0]),
+        pltpu.make_async_copy(down, factor, sems.at[1]),
+    ]
+    for k in range(SPLITS):
+        rows = pl.ds(k * piece, piece)
+        fetches.append(pltpu.make_async_copy(cache.at[rows], held.at[rows], sems.at[2 + k]))
+    for fetch in fetches:
+        fetch.start()
+    fetches[0].wait()
+    fetches[1].wait()
     part = lax.dot_general(
-        hidden[:, own], down[...], (((1,), (1,)), ((), ())), preferred_element_type=jnp.float32
+        some[...], factor[...], (((1,), (1,)), ((), ())), preferred_element_type=jnp.float32
     )
     high = part.astype(jnp.bfloat16).astype(jnp.float32)
     terms = jnp.concatenate([high, part - high], axis=1).astype(jnp.bfloat16)
-    share = cache.shape[0] // BLOCK
-    for head in range(KEY_VALUE_HEADS):
-        columns = slice(head * HEAD_WIDTH, (head + 1) * HEAD_WIDTH)
-        for d in range(BLOCK):
-            to = head * BLOCK + d
-            out[to, :share] = cache[d * share : (d + 1) * share, :, columns]
-            for t in range(DECODE_STEPS):
-                out[to, share + t // 2, t % 2, :] = terms[t]
+    stores = []
+    each = BLOCK // SPLITS
+    for k in range(SPLITS):
+        fetches[2 + k].wait()
+        for d in range(k * each, (k + 1) * each):
+            for head in range(KEY_VALUE_HEADS):
+                columns = slice(head * HEAD_WIDTH, (head + 1) * HEAD_WIDTH)
+                ready[head, d, :share] = held[d * share : (d + 1) * share, :, columns]
+                for t in range(DECODE_STEPS):
+                    ready[head, d, share + t // 2, t % 2, :] = terms[t]
+        rows = pl.ds(k * each, each)
+        stores.append(
+            pltpu.make_async_copy(ready.at[:, rows], out.at[:, rows], sems.at[2 + SPLITS + k])
+        )
+        stores[-1].start()
+    for store in stores:
+        store.wait()
 
 
 def attend_kernel(
@@ -168,15 +193,26 @@
     smem = pl.BlockSpec(memory_space=pltpu.SMEM)
     everyone = ("role",) + plane
     share = cache.shape[1] // BLOCK
+    sent = jax.ShapeDtypeStruct(
+        (KEY_VALUE_HEADS, BLOCK, share + DECODE_STEPS // 2, 2, HEAD_WIDTH), cache.dtype
+    )
+    hbm = pl.BlockSpec(memory_space=pl.ANY)
     sent = pl.pallas_call(
         split_kernel,
-        out_shape=jax.ShapeDtypeStruct(
-            (lax.axis_size(everyone), share + DECODE_STEPS // 2, 2, HEAD_WIDTH), cache.dtype
-        ),
-        in_specs=[smem] + [vmem] * 3,
-        out_specs=vmem,
+        out_shape=sent,
+        in_specs=[smem] + [hbm] * 3,
+        out_specs=hbm,
+        scratch_shapes=[
+            pltpu.VMEM((rows.shape[0], down.shape[1]), rows.dtype),
+            pltpu.VMEM(down.shape, down.dtype),
+            pltpu.VMEM(cache.shape[1:], cache.dtype),
+            pltpu.VMEM(sent.shape, sent.dtype),
+            pltpu.SemaphoreType.DMA((2 + 2 * SPLITS,)),
+        ],
+        compiler_params=pltpu.CompilerParams(vmem_limit_bytes=58 * 2**20),
         name="split",
     )(shard[None].astype(jnp.int32), rows, down, cache[0])
+    sent = sent.reshape((-1,) + sent.shape[2:])
     cached = lax.all_to_all(sent, everyone, 0, 0)
     rows_each = 2 * cached.shape[1]
     cached = cached.reshape(-1, HEAD_WIDTH)

time: 50.7 us -> 50.5 us (level)
  no operation moved by 1% of the time
where the time goes in v6:
time: 50.5 us; the launch traced here: 50.3 us
  starting transfers between devices  17.8 us (35%)
  blocking collectives  10.9 us (22%)
  waiting for transfers between devices  10.6 us (21%)
  matrix products  4.65 us (9%)
  Pallas kernels  4.35 us (9%)
  other arithmetic  1.17 us (2%)
  between operations  0.75 us (1%)
    all_to_all x1, starting transfers between devices, local(): cached = lax.all_to_all(sent, everyone, 0, 0)  13.7 us
    all_to_all x1, blocking collectives, local(): parts = lax.all_to_all(parts, block, 0, 0)  8.98 us
    ppermute x3, waiting for transfers between devices, swapped(): return lax.ppermute(block, axis, [(i, i ^ apart) for i in range(count)])  8.27 us
    dot_general x1, matrix products, local(): base = jnp.dot(rows, current_weight, preferred_element_type=jnp.float32)  4.65 us
    ppermute x3, starting transfers between devices, swapped(): return lax.ppermute(block, axis, [(i, i ^ apart) for i in range(count)])  4.1 us
    all_to_all x1, waiting for transfers between devices, local(): cached = lax.all_to_all(sent, everyone, 0, 0)  2.35 us
    pallas_call x1, Pallas kernels, local(): pl.pallas_call(split_kernel, out_shape=sent, in_specs=[smem] + [hbm] * 3,...  2.35 us
    pallas_call x1, Pallas kernels, local(): pl.pallas_call(attend_kernel, out_shape=jax.ShapeDtypeStruct((BLOCK, 6 *...  2 us
  transfers between devices with their start and end apart: 4, of which 4 were waited for; matrix products, arithmetic and copies ran while one was open for 10% of the time, Pallas kernels for 0%

profile of v6, /device:TPU:32, one launch (start us, length us, event | category | flops | bytes accessed | tf_op | source)
XLA Modules:
  0.0 50.3 jit_solution(13539411533586665523)
XLA Ops:
  0.0 0.0 copy-start.1
  0.0 0.0 copy-start
  0.0 2.3 %split.1 = bf16[8,8,18,2,128]{4,3,2,1,0:T(2,128)(2,1)} custom-call(s32[1]{0:T(128)} %bitcast.4.info, bf16[4,16384]{1,0:T(4,128)(2,1)} %bitcast.181, bf16[64,512]{1,0:T(8,128)(2,1)} %bitcast.184, bf16[128,2,1024]{2,1,0:T(2,128)(2,1)} %bitcast.183), custom_call_target="tpu_custom_call" | custom-call | tf_op jit(solution)/shard_map/split/pallas_call | solution.py:200
  2.4 13.7 %all-to-all-start = ((bf16[64,18,2,128]{3,2,1,0:T(2,128)(2,1)}), bf16[64,18,2,128]{3,2,1,0:T(2,128)(2,1)S(1)}, u32[]{:S(2)}, u32[]{:S(2)}) async-start(bf16[64,18,2,128]{3,2,1,0:T(2,128)(2,1)} %bitcast.180), calls=%async_computation | async-start | bytes 1179648 | tf_op jit(solution)/shard_map/all_to_all | solution.py:216
  16.0 4.7 %fusion.11 = (bf16[4,256]{1,0:T(4,128)(2,1)S(1)}, bf16[4,256]{1,0:T(4,128)(2,1)S(1)}, bf16[4,256]{1,0:T(4,128)(2,1)S(1)}) fusion(bf16[4,16384]{1,0:T(4,128)(2,1)} %bitcast.182, bf16[16384,256]{1,0:T(8,128)(2,1)} %param.8), kind=kOutput, calls=%fused_computation.33 | convolution fusion | flops 33561600 | bytes 8525824 | tf_op jit(solution)/shard_map/dot_general | solution.py:230
  20.7 0.0 copy-done.1
  20.7 0.1 concatenate.12
  20.8 1.9 %all_gather.3.up0 = bf16[288,256]{1,0:T(8,128)(2,1)S(1)} all-gather(bf16[144,256]{1,0:T(8,128)(2,1)S(1)} %concatenate.12), channel_id=1, replica_groups=mesh['role'=2,'grp'=4,'y'=4,'x'=4,'core'=2] {'core'}, dimensions={0}, use_global_device_ids=true | all-gather | bytes 221184 | tf_op jit(solution)/shard_map/all_gather | solution.py:236
  22.7 2.8 %collective-permute-start.2 = (bf16[288,256]{1,0:T(8,128)(2,1)S(1)}, bf16[288,256]{1,0:T(8,128)(2,1)S(1)}, u32[]{:S(2)}, u32[]{:S(2)}) collective-permute-start(bf16[288,256]{1,0:T(8,128)(2,1)S(1)} %all_gather.3.up0), channel_id=1, source_target_pairs={{0,6},{2,4},{4,2},{6,0},{1,7},{3,5},{5,3},{7,1},{8,14},{10,12},{12... | collective-permute-start | bytes 442376 | tf_op jit(solution)/shard_map/ppermute | solution.py:33
  25.5 0.9 %collective-permute-start.1 = (bf16[288,256]{1,0:T(8,128)(2,1)S(1)}, bf16[288,256]{1,0:T(8,128)(2,1)S(1)}, u32[]{:S(2)}, u32[]{:S(2)}) collective-permute-start(bf16[288,256]{1,0:T(8,128)(2,1)S(1)} %all_gather.3.up0), channel_id=1, source_target_pairs={{0,4},{2,6},{4,0},{6,2},{1,5},{3,7},{5,1},{7,3},{8,12},{10,14},{12... | collective-permute-start | bytes 442376 | tf_op jit(solution)/shard_map/ppermute | solution.py:33
  26.3 0.5 collective-permute-start
  27.5 0.1 multiply_cosine_fusion
  27.6 0.1 maximum_bitcast_fusion
  27.7 0.1 and_select_fusion.2.pos
  27.8 0.1 select_convert_fusion.pick
  27.9 0.1 pad_add_fusion.info
  28.0 6.7 %collective-permute-done.2.up3 = bf16[288,256]{1,0:T(8,128)(2,1)S(1)} collective-permute-done((bf16[288,256]{1,0:T(8,128)(2,1)S(1)}, bf16[288,256]{1,0:T(8,128)(2,1)S(1)}, u32[]{:S(2)}, u32[]{:S(2)}) %collective-permute-start.2) | collective-permute-done | bytes 147488 | tf_op jit(solution)/shard_map/ppermute | solution.py:33
  34.7 0.5 collective-permute-done.1.up2
  35.2 1.1 %collective-permute-done.up1 = bf16[288,256]{1,0:T(8,128)(2,1)S(1)} collective-permute-done((bf16[288,256]{1,0:T(8,128)(2,1)S(1)}, bf16[288,256]{1,0:T(8,128)(2,1)S(1)}, u32[]{:S(2)}, u32[]{:S(2)}) %collective-permute-start) | collective-permute-done | bytes 147488 | tf_op jit(solution)/shard_map/ppermute | solution.py:33
  36.3 2.4 %all-to-all-done = bf16[64,18,2,128]{3,2,1,0:T(2,128)(2,1)S(1)} async-done(((bf16[64,18,2,128]{3,2,1,0:T(2,128)(2,1)}), bf16[64,18,2,128]{3,2,1,0:T(2,128)(2,1)S(1)}, u32[]{:S(2)}, u32[]{:S(2)}) %all-to-all-start) | async-done | bytes 589856 | tf_op jit(solution)/shard_map/all_to_all | solution.py:216
  38.7 0.0 copy-done
  38.7 2.0 %attend.1 = f32[8,24,128]{2,1,0:T(8,128)S(1)} custom-call(s32[3]{0:T(128)S(1)} %pad_add_fusion.info, s32[1,2304]{1,0:T(1,128)S(1)} %and_select_fusion.2.pos, bf16[16,2304]{1,0:T(8,128)(2,1)S(1)} %select_convert_fusion.pick, bf16[288,256]{1,0:T(8,128)(2,1)S(1)} %all_gather.3.up0, bf16[288,256]{1,0:T(8,128)(2,1)S(1)} %collective-permute-done.up1, ...), custom_call_target="tpu_custom_call" | custom-call | tf_op jit(solution)/shard_map/attend/pallas_call | solution.py:249
  40.7 9.0 %all_to_all.10 = f32[8,24,128]{2,1,0:T(8,128)S(1)} all-to-all(f32[8,24,128]{2,1,0:T(8,128)S(1)} %attend.1), channel_id=1, replica_groups=mesh['role'=2,'grp'=4,'y'=4,'x'=4,'core'=2] {'x','core'}, dimensions={0} | all-to-all | bytes 196608 | tf_op jit(solution)/shard_map/all_to_all | solution.py:258
  49.7 0.6 %maximum_bitcast_fusion.2 = bf16[4,1,256]{2,0,1:T(4,128)(2,1)} fusion(bf16[4,128]{1,0:T(4,128)(2,1)S(1)} %get-tuple-element.11, bf16[4,128]{1,0:T(4,128)(2,1)S(1)} %get-tuple-element.10), kind=kLoop, calls=%fused_computation.95 | loop fusion | flops 4096 | bytes 4096 | tf_op jit(solution)/shard_map/broadcast_in_dim | solution.py:260
  (10 shorter events, 0.1 us)
Async XLA Ops:
  0.0 20.7 %copy-start.1 = (bf16[2,1,64,256]{3,2,1,0:T(8,128)(2,1)S(1)}, bf16[2,1,64,256]{3,2,1,0:T(8,128)(2,1)}, u32[]{:S(2)}) copy-start(bf16[2,1,64,256]{3,2,1,0:T(8,128)(2,1)} %param.10) | copy-start | bytes 196612
  0.0 38.7 %copy-start = (bf16[4,1,2,1024]{3,2,1,0:T(2,128)(2,1)S(1)}, bf16[4,1,2,1024]{3,2,1,0:T(2,128)(2,1)}, u32[]{:S(2)}) copy-start(bf16[4,1,2,1024]{3,2,1,0:T(2,128)(2,1)} %newest.1) | copy-start | bytes 49156
  2.4 36.3 %all-to-all-start = ((bf16[64,18,2,128]{3,2,1,0:T(2,128)(2,1)}), bf16[64,18,2,128]{3,2,1,0:T(2,128)(2,1)S(1)}, u32[]{:S(2)}, u32[]{:S(2)}) async-start(bf16[64,18,2,128]{3,2,1,0:T(2,128)(2,1)} %bitcast.180), calls=%async_computation | async-start | bytes 1179648 | tf_op jit(solution)/shard_map/all_to_all | solution.py:216
  22.7 12.0 %collective-permute-start.2 = (bf16[288,256]{1,0:T(8,128)(2,1)S(1)}, bf16[288,256]{1,0:T(8,128)(2,1)S(1)}, u32[]{:S(2)}, u32[]{:S(2)}) collective-permute-start(bf16[288,256]{1,0:T(8,128)(2,1)S(1)} %all_gather.3.up0), channel_id=1, source_target_pairs={{0,6},{2,4},{4,2},{6,0},{1,7},{3,5},{5,3},{7,1},{8,14},{10,12},{12... | collective-permute-start | bytes 442376 | tf_op jit(solution)/shard_map/ppermute | solution.py:33
  25.5 9.7 %collective-permute-start.1 = (bf16[288,256]{1,0:T(8,128)(2,1)S(1)}, bf16[288,256]{1,0:T(8,128)(2,1)S(1)}, u32[]{:S(2)}, u32[]{:S(2)}) collective-permute-start(bf16[288,256]{1,0:T(8,128)(2,1)S(1)} %all_gather.3.up0), channel_id=1, source_target_pairs={{0,4},{2,6},{4,0},{6,2},{1,5},{3,7},{5,1},{7,3},{8,12},{10,14},{12... | collective-permute-start | bytes 442376 | tf_op jit(solution)/shard_map/ppermute | solution.py:33
  26.3 10.0 %collective-permute-start = (bf16[288,256]{1,0:T(8,128)(2,1)S(1)}, bf16[288,256]{1,0:T(8,128)(2,1)S(1)}, u32[]{:S(2)}, u32[]{:S(2)}) collective-permute-start(bf16[288,256]{1,0:T(8,128)(2,1)S(1)} %all_gather.3.up0), channel_id=1, source_target_pairs={{0,2},{2,0},{4,6},{6,4},{1,3},{3,1},{5,7},{7,5},{8,10},{10,8},{12,... | collective-permute-start | bytes 442376 | tf_op jit(solution)/shard_map/ppermute | solution.py:33

commit v7 on v6

--- a/solution.py
+++ b/solution.py
@@ -122,7 +122,7 @@
     fresh_value = jnp.concatenate(
         [newest[:, 0, 1, own].astype(jnp.float32), blank], axis=0
     ).astype(jnp.bfloat16)
-    chunk = 256
+    chunk = 768
     n_src = cached.shape[0] // chunk
     blocks = [slice(j * chunk, (j + 1) * chunk) for j in range(n_src)]
     row = lax.broadcasted_iota(jnp.int32, (ROWS, HEAD_WIDTH), 0)

time: 50.5 us -> 50.3 us (level)
  transfers between devices with their start and end apart: 4 -> 4, of which waited for: 4 -> 4; matrix products, arithmetic and copies ran while one was open for 10% -> 11% of each run, Pallas kernels for 0% -> 0%
where the time goes in v7:
time: 50.3 us; the launch traced here: 50.1 us
  starting transfers between devices  17.8 us (35%)
  blocking collectives  10.9 us (22%)
  waiting for transfers between devices  10.6 us (21%)
  matrix products  4.65 us (9%)
  Pallas kernels  4.14 us (8%)
  other arithmetic  1.17 us (2%)
  between operations  0.75 us (1%)
    all_to_all x1, starting transfers between devices, local(): cached = lax.all_to_all(sent, everyone, 0, 0)  13.7 us
    all_to_all x1, blocking collectives, local(): parts = lax.all_to_all(parts, block, 0, 0)  8.99 us
    ppermute x3, waiting for transfers between devices, swapped(): return lax.ppermute(block, axis, [(i, i ^ apart) for i in range(count)])  8.27 us
    dot_general x1, matrix products, local(): base = jnp.dot(rows, current_weight, preferred_element_type=jnp.float32)  4.65 us
    ppermute x3, starting transfers between devices, swapped(): return lax.ppermute(block, axis, [(i, i ^ apart) for i in range(count)])  4.1 us
    all_to_all x1, waiting for transfers between devices, local(): cached = lax.all_to_all(sent, everyone, 0, 0)  2.35 us
    pallas_call x1, Pallas kernels, local(): pl.pallas_call(split_kernel, out_shape=sent, in_specs=[smem] + [hbm] * 3,...  2.35 us
    all_gather x1, blocking collectives, local(): up = lax.all_gather(up, 'core', axis=0, tiled=True)  1.9 us
  transfers between devices with their start and end apart: 4, of which 4 were waited for; matrix products, arithmetic and copies ran while one was open for 11% of the time, Pallas kernels for 0%

profile of v7, /device:TPU:32, one launch (start us, length us, event | category | flops | bytes accessed | tf_op | source)
XLA Modules:
  0.0 50.1 jit_solution(12180956689182677169)
XLA Ops:
  0.0 0.0 copy-start.1
  0.0 0.0 copy-start
  0.0 2.3 %split.1 = bf16[8,8,18,2,128]{4,3,2,1,0:T(2,128)(2,1)} custom-call(s32[1]{0:T(128)} %bitcast.4.info, bf16[4,16384]{1,0:T(4,128)(2,1)} %bitcast.181, bf16[64,512]{1,0:T(8,128)(2,1)} %bitcast.184, bf16[128,2,1024]{2,1,0:T(2,128)(2,1)} %bitcast.183), custom_call_target="tpu_custom_call" | custom-call | tf_op jit(solution)/shard_map/split/pallas_call | solution.py:200
  2.4 13.7 %all-to-all-start = ((bf16[64,18,2,128]{3,2,1,0:T(2,128)(2,1)}), bf16[64,18,2,128]{3,2,1,0:T(2,128)(2,1)S(1)}, u32[]{:S(2)}, u32[]{:S(2)}) async-start(bf16[64,18,2,128]{3,2,1,0:T(2,128)(2,1)} %bitcast.180), calls=%async_computation | async-start | bytes 1179648 | tf_op jit(solution)/shard_map/all_to_all | solution.py:216
  16.0 4.7 %fusion.11 = (bf16[4,256]{1,0:T(4,128)(2,1)S(1)}, bf16[4,256]{1,0:T(4,128)(2,1)S(1)}, bf16[4,256]{1,0:T(4,128)(2,1)S(1)}) fusion(bf16[4,16384]{1,0:T(4,128)(2,1)} %bitcast.182, bf16[16384,256]{1,0:T(8,128)(2,1)} %param.8), kind=kOutput, calls=%fused_computation.33 | convolution fusion | flops 33561600 | bytes 8525824 | tf_op jit(solution)/shard_map/dot_general | solution.py:230
  20.7 0.0 copy-done.1
  20.7 0.1 concatenate.12
  20.8 1.9 %all_gather.3.up0 = bf16[288,256]{1,0:T(8,128)(2,1)S(1)} all-gather(bf16[144,256]{1,0:T(8,128)(2,1)S(1)} %concatenate.12), channel_id=1, replica_groups=mesh['role'=2,'grp'=4,'y'=4,'x'=4,'core'=2] {'core'}, dimensions={0}, use_global_device_ids=true | all-gather | bytes 221184 | tf_op jit(solution)/shard_map/all_gather | solution.py:236
  22.7 2.8 %collective-permute-start.2 = (bf16[288,256]{1,0:T(8,128)(2,1)S(1)}, bf16[288,256]{1,0:T(8,128)(2,1)S(1)}, u32[]{:S(2)}, u32[]{:S(2)}) collective-permute-start(bf16[288,256]{1,0:T(8,128)(2,1)S(1)} %all_gather.3.up0), channel_id=1, source_target_pairs={{0,6},{2,4},{4,2},{6,0},{1,7},{3,5},{5,3},{7,1},{8,14},{10,12},{12... | collective-permute-start | bytes 442376 | tf_op jit(solution)/shard_map/ppermute | solution.py:33
  25.5 0.9 %collective-permute-start.1 = (bf16[288,256]{1,0:T(8,128)(2,1)S(1)}, bf16[288,256]{1,0:T(8,128)(2,1)S(1)}, u32[]{:S(2)}, u32[]{:S(2)}) collective-permute-start(bf16[288,256]{1,0:T(8,128)(2,1)S(1)} %all_gather.3.up0), channel_id=1, source_target_pairs={{0,4},{2,6},{4,0},{6,2},{1,5},{3,7},{5,1},{7,3},{8,12},{10,14},{12... | collective-permute-start | bytes 442376 | tf_op jit(solution)/shard_map/ppermute | solution.py:33
  26.3 0.5 collective-permute-start
  27.5 0.1 multiply_cosine_fusion
  27.6 0.1 maximum_bitcast_fusion
  27.7 0.1 and_select_fusion.2.pos
  27.8 0.1 select_convert_fusion.pick
  27.9 0.1 pad_add_fusion.info
  28.0 6.7 %collective-permute-done.2.up3 = bf16[288,256]{1,0:T(8,128)(2,1)S(1)} collective-permute-done((bf16[288,256]{1,0:T(8,128)(2,1)S(1)}, bf16[288,256]{1,0:T(8,128)(2,1)S(1)}, u32[]{:S(2)}, u32[]{:S(2)}) %collective-permute-start.2) | collective-permute-done | bytes 147488 | tf_op jit(solution)/shard_map/ppermute | solution.py:33
  34.7 0.5 collective-permute-done.1.up2
  35.2 1.1 %collective-permute-done.up1 = bf16[288,256]{1,0:T(8,128)(2,1)S(1)} collective-permute-done((bf16[288,256]{1,0:T(8,128)(2,1)S(1)}, bf16[288,256]{1,0:T(8,128)(2,1)S(1)}, u32[]{:S(2)}, u32[]{:S(2)}) %collective-permute-start) | collective-permute-done | bytes 147488 | tf_op jit(solution)/shard_map/ppermute | solution.py:33
  36.3 2.4 %all-to-all-done = bf16[64,18,2,128]{3,2,1,0:T(2,128)(2,1)S(1)} async-done(((bf16[64,18,2,128]{3,2,1,0:T(2,128)(2,1)}), bf16[64,18,2,128]{3,2,1,0:T(2,128)(2,1)S(1)}, u32[]{:S(2)}, u32[]{:S(2)}) %all-to-all-start) | async-done | bytes 589856 | tf_op jit(solution)/shard_map/all_to_all | solution.py:216
  38.7 0.0 copy-done
  38.7 1.8 %attend.1 = f32[8,24,128]{2,1,0:T(8,128)S(1)} custom-call(s32[3]{0:T(128)S(1)} %pad_add_fusion.info, s32[1,2304]{1,0:T(1,128)S(1)} %and_select_fusion.2.pos, bf16[16,2304]{1,0:T(8,128)(2,1)S(1)} %select_convert_fusion.pick, bf16[288,256]{1,0:T(8,128)(2,1)S(1)} %all_gather.3.up0, bf16[288,256]{1,0:T(8,128)(2,1)S(1)} %collective-permute-done.up1, ...), custom_call_target="tpu_custom_call" | custom-call | tf_op jit(solution)/shard_map/attend/pallas_call | solution.py:249
  40.5 9.0 %all_to_all.10 = f32[8,24,128]{2,1,0:T(8,128)S(1)} all-to-all(f32[8,24,128]{2,1,0:T(8,128)S(1)} %attend.1), channel_id=1, replica_groups=mesh['role'=2,'grp'=4,'y'=4,'x'=4,'core'=2] {'x','core'}, dimensions={0} | all-to-all | bytes 196608 | tf_op jit(solution)/shard_map/all_to_all | solution.py:258
  49.5 0.6 %maximum_bitcast_fusion.2 = bf16[4,1,256]{2,0,1:T(4,128)(2,1)} fusion(bf16[4,128]{1,0:T(4,128)(2,1)S(1)} %get-tuple-element.11, bf16[4,128]{1,0:T(4,128)(2,1)S(1)} %get-tuple-element.10), kind=kLoop, calls=%fused_computation.95 | loop fusion | flops 4096 | bytes 4096 | tf_op jit(solution)/shard_map/broadcast_in_dim | solution.py:260
  (10 shorter events, 0.1 us)
Async XLA Ops:
  0.0 20.7 %copy-start.1 = (bf16[2,1,64,256]{3,2,1,0:T(8,128)(2,1)S(1)}, bf16[2,1,64,256]{3,2,1,0:T(8,128)(2,1)}, u32[]{:S(2)}) copy-start(bf16[2,1,64,256]{3,2,1,0:T(8,128)(2,1)} %param.10) | copy-start | bytes 196612
  0.0 38.7 %copy-start = (bf16[4,1,2,1024]{3,2,1,0:T(2,128)(2,1)S(1)}, bf16[4,1,2,1024]{3,2,1,0:T(2,128)(2,1)}, u32[]{:S(2)}) copy-start(bf16[4,1,2,1024]{3,2,1,0:T(2,128)(2,1)} %newest.1) | copy-start | bytes 49156
  2.4 36.3 %all-to-all-start = ((bf16[64,18,2,128]{3,2,1,0:T(2,128)(2,1)}), bf16[64,18,2,128]{3,2,1,0:T(2,128)(2,1)S(1)}, u32[]{:S(2)}, u32[]{:S(2)}) async-start(bf16[64,18,2,128]{3,2,1,0:T(2,128)(2,1)} %bitcast.180), calls=%async_computation | async-start | bytes 1179648 | tf_op jit(solution)/shard_map/all_to_all | solution.py:216
  22.7 12.0 %collective-permute-start.2 = (bf16[288,256]{1,0:T(8,128)(2,1)S(1)}, bf16[288,256]{1,0:T(8,128)(2,1)S(1)}, u32[]{:S(2)}, u32[]{:S(2)}) collective-permute-start(bf16[288,256]{1,0:T(8,128)(2,1)S(1)} %all_gather.3.up0), channel_id=1, source_target_pairs={{0,6},{2,4},{4,2},{6,0},{1,7},{3,5},{5,3},{7,1},{8,14},{10,12},{12... | collective-permute-start | bytes 442376 | tf_op jit(solution)/shard_map/ppermute | solution.py:33
  25.5 9.7 %collective-permute-start.1 = (bf16[288,256]{1,0:T(8,128)(2,1)S(1)}, bf16[288,256]{1,0:T(8,128)(2,1)S(1)}, u32[]{:S(2)}, u32[]{:S(2)}) collective-permute-start(bf16[288,256]{1,0:T(8,128)(2,1)S(1)} %all_gather.3.up0), channel_id=1, source_target_pairs={{0,4},{2,6},{4,0},{6,2},{1,5},{3,7},{5,1},{7,3},{8,12},{10,14},{12... | collective-permute-start | bytes 442376 | tf_op jit(solution)/shard_map/ppermute | solution.py:33
  26.3 10.0 %collective-permute-start = (bf16[288,256]{1,0:T(8,128)(2,1)S(1)}, bf16[288,256]{1,0:T(8,128)(2,1)S(1)}, u32[]{:S(2)}, u32[]{:S(2)}) collective-permute-start(bf16[288,256]{1,0:T(8,128)(2,1)S(1)} %all_gather.3.up0), channel_id=1, source_target_pairs={{0,2},{2,0},{4,6},{6,4},{1,3},{3,1},{5,7},{7,5},{8,10},{10,8},{12,... | collective-permute-start | bytes 442376 | tf_op jit(solution)/shard_map/ppermute | solution.py:33
